TPU v7x, 512 devices: a whole 4x8x8 slice. The times are simulated.
512 devices in a mesh: users: 64 (over z, x, core), ctx: 8 (over y).
Axes of the slice: x: 4, y: 8, z: 8, core: 2. Of those that a mesh axis runs over, the one named last changes fastest.
Arguments:
- events: bfloat16 [32768, 1024], P(('users', 'ctx')), may hold values from -6 to 6
- owner_id: int32 [32768, 1], P(('users', 'ctx')), may hold values from 0 to 63; in each aligned block of 64 rows (0 to 63, 64 to 127, ...) at most 2 rows name the same one
- event_bucket: int32 [32768], P(('users', 'ctx')), may hold values from 0 to 31
- cross_weight: bfloat16 [1024, 1024], P('users'), may hold values from -0.1875 to 0.1875
- cross_bias: float32 [1024], replicated, may hold values from -3 to 3
- project_weight: bfloat16 [1024, 4096], P('users'), may hold values from -0.1875 to 0.1875
- cache_keys: bfloat16 [64, 8192, 1024], P('users', 'ctx'), may hold values from -6 to 6
- cache_values: bfloat16 [64, 8192, 1024], P('users', 'ctx'), may hold values from -60 to 60
- cache_length: int32 [64], P('users'), may hold values from 1024 to 8192
- cache_bucket: int32 [64, 8192], P('users', 'ctx'), may hold values from 0 to 31
- time_bias: float32 [32, 8], replicated, may hold values from -3 to 3
- norm_gain: float32 [1024], replicated, may hold values from 0.1 to 1.9
Outputs:
- gated: bfloat16 [32768, 1024], P(('users', 'ctx'))
Inputs may be any that keep to these rules, and one draw needn't show every extreme that they name: `owner_id`: no user is named by more than 2 of the 64 rows of one ingestion shard, and some user reaches that.
All inputs are finite; a program needn't handle non-finite values.
Results may differ from a plain program's by a relative error of at most 0.035.
Values may be sent and summed in bfloat16 or wider, within the bound.
A program may use at most 64 MiB of HBM per device.

v0:
```python
import jax
import jax.numpy as jnp
from jax import lax
from jax.sharding import PartitionSpec as P

H = 8


norm_epsilon = 1e-05


def from_everyone(value, axis):
    copies = jnp.broadcast_to(value, (lax.axis_size(axis), *value.shape))
    return lax.all_to_all(copies, axis, split_axis=0, concat_axis=0, tiled=True)


def in_order(parts, dim):
    parts = jnp.moveaxis(parts, 0, dim)
    dims = parts.shape
    return parts.reshape(*dims[:dim], dims[dim] * dims[dim + 1], *dims[dim + 2 :])


def gather_directly(value, axis, dim):
    parts = from_everyone(value, axis)
    return in_order(parts, dim)


def split_up(value, dim, peers):
    before, after = (value.shape[:dim], value.shape[dim + 1 :])
    return jnp.moveaxis(value.reshape(*before, peers, -1, *after), dim, 0)


def summed_on_arrival(value, axis, dim):
    parts = split_up(value, dim, lax.axis_size(axis))
    arrived = lax.all_to_all(parts, axis, split_axis=0, concat_axis=0, tiled=True)
    return arrived.astype(jnp.float32).sum(axis=0)


def bias_table(buckets, time_bias):
    levels = jnp.arange(time_bias.shape[0], dtype=jnp.int32)
    picked = (buckets[:, None] == levels[None, :]).astype(jnp.float32)
    return jnp.dot(picked, time_bias, precision=lax.Precision.HIGHEST)


def weighted_sum(keys_part, values_part, queries, key_bias, allowed, scale_factor):
    scores = jnp.einsum("khd,qhd->hkq", keys_part, queries, preferred_element_type=jnp.float32)
    scores = scores * scale_factor + key_bias.T[:, :, None]
    weights = jnp.where(allowed, jax.nn.silu(scores), 0.0).astype(jnp.bfloat16)
    return jnp.einsum("hkq,khd->qhd", weights, values_part, preferred_element_type=jnp.float32)


def shards(
    events,
    owner_id,
    event_bucket,
    cross_weight,
    cross_bias,
    project_weight,
    cache_keys,
    cache_values,
    cache_length,
    cache_bucket,
    time_bias,
    norm_gain,
):
    row_count, feature_width = events.shape
    head_count = H
    head_width = feature_width // head_count
    owner_count = lax.axis_size("users")
    context_count = lax.axis_size("ctx")
    context_index = lax.axis_index("ctx")
    capacity = max(2, (3 * row_count + 2 * owner_count - 1) // (2 * owner_count))
    slot_count = owner_count * capacity
    cache_rows = cache_keys.shape[1]
    scale_factor = head_width ** (-0.5)
    source = events.astype(jnp.float32)
    cross_full = gather_directly(cross_weight, "users", 0)
    crossing = jnp.dot(events, cross_full, preferred_element_type=jnp.float32)
    crossed = (source * (crossing + cross_bias) + source).astype(jnp.bfloat16)
    owners = owner_id[:, 0]
    positions = jnp.arange(row_count, dtype=jnp.int32)
    earlier = (owners[None, :] == owners[:, None]) & (positions[None, :] < positions[:, None])
    ranking = jnp.sum(earlier.astype(jnp.int32), axis=1)
    slot_of_row = owners * capacity + ranking
    placing = jnp.arange(slot_count, dtype=jnp.int32)[:, None] == slot_of_row[None, :]
    placing_matrix = placing.astype(jnp.bfloat16)
    outgoing = jnp.dot(placing_matrix, crossed, preferred_element_type=jnp.float32).astype(
        jnp.bfloat16
    )
    labels = jnp.sum(jnp.where(placing, event_bucket[None, :] + 1, 0), axis=1).astype(jnp.bfloat16)
    arrived, arrived_labels = (
        lax.all_to_all(
            outgoing.reshape(owner_count, capacity, feature_width),
            "users",
            split_axis=0,
            concat_axis=0,
            tiled=True,
        ),
        lax.all_to_all(
            labels.reshape(owner_count, capacity), "users", split_axis=0, concat_axis=0, tiled=True
        ),
    )
    arrived = arrived.reshape(slot_count, feature_width)
    label_values = arrived_labels.reshape(slot_count).astype(jnp.int32)
    project_full = lax.all_gather(project_weight, "users", axis=0, tiled=True)
    projected = jnp.dot(arrived, project_full, preferred_element_type=jnp.float32)
    activated = jax.nn.silu(projected)
    gate_units = activated[:, :feature_width].astype(jnp.bfloat16)
    new_values = (
        activated[:, feature_width : 2 * feature_width]
        .astype(jnp.bfloat16)
        .reshape(slot_count, head_count, head_width)
    )
    new_queries = activated[:, 2 * feature_width : 3 * feature_width].astype(jnp.bfloat16)
    new_keys = (
        activated[:, 3 * feature_width :]
        .astype(jnp.bfloat16)
        .reshape(slot_count, head_count, head_width)
    )
    slot_index = jnp.arange(slot_count, dtype=jnp.int32)
    key_order = (
        slot_index // capacity * context_count + context_index
    ) * capacity + slot_index % capacity
    key_valid = label_values > 0
    new_bias = bias_table(jnp.maximum(label_values - 1, 0), time_bias)
    cache_key_heads = cache_keys[0].reshape(cache_rows, head_count, head_width)
    cache_value_heads = cache_values[0].reshape(cache_rows, head_count, head_width)
    cache_bias = bias_table(cache_bucket[0], time_bias)
    live_length = cache_length[0] - context_index * cache_rows
    cache_live = jnp.arange(cache_rows, dtype=jnp.int32) < live_length
    block_keys = min(256, cache_rows)
    block_total = cache_rows // block_keys

    def attend_block(query_rows, query_start):
        block_rows = query_rows.shape[0]
        queries = query_rows.reshape(block_rows, head_count, head_width)
        query_index = query_start + jnp.arange(block_rows, dtype=jnp.int32)
        query_context = query_index // slot_count
        query_slot = query_index % slot_count
        query_order = (
            query_slot // capacity * context_count + query_context
        ) * capacity + query_slot % capacity
        allowed = key_valid[None, :, None] & (
            key_order[None, :, None] <= query_order[None, None, :]
        )
        summed = weighted_sum(new_keys, new_values, queries, new_bias, allowed, scale_factor)

        def add_block(block_number, carried):
            offset = block_number * block_keys
            keys_part = lax.dynamic_slice_in_dim(cache_key_heads, offset, block_keys, 0)
            values_part = lax.dynamic_slice_in_dim(cache_value_heads, offset, block_keys, 0)
            bias_part = lax.dynamic_slice_in_dim(cache_bias, offset, block_keys, 0)
            live_part = lax.dynamic_slice_in_dim(cache_live, offset, block_keys, 0)
            return carried + weighted_sum(
                keys_part, values_part, queries, bias_part, live_part[None, :, None], scale_factor
            )

        summed = lax.fori_loop(0, block_total, add_block, summed)
        return summed.reshape(block_rows, feature_width)

    query_piece = lax.all_gather(new_queries, "ctx", axis=0, tiled=True)
    piece_rows = query_piece.shape[0]
    block_count = piece_rows // 512
    stacked = query_piece.reshape(block_count, 512, feature_width)
    block_starts = 512 * jnp.arange(block_count, dtype=jnp.int32)

    def one_block(bundle):
        return attend_block(bundle[0], bundle[1])

    outputs = lax.map(one_block, (stacked, block_starts))
    partials = outputs.reshape(piece_rows, feature_width)
    attended = summed_on_arrival(partials.astype(jnp.bfloat16), "ctx", 0)
    center = jnp.mean(attended, axis=1, keepdims=True)
    spread = jnp.mean(jnp.square(attended - center), axis=1, keepdims=True)
    normed = (attended - center) * lax.rsqrt(spread + norm_epsilon)
    gated = (normed * norm_gain * gate_units.astype(jnp.float32)).astype(jnp.bfloat16)
    returned = lax.all_to_all(
        gated.reshape(owner_count, capacity, feature_width),
        "users",
        split_axis=0,
        concat_axis=0,
        tiled=True,
    )
    result = lax.dot_general(
        placing_matrix,
        returned.reshape(slot_count, feature_width),
        (((0,), (0,)), ((), ())),
        preferred_element_type=jnp.float32,
    )
    return result.astype(jnp.bfloat16)


def solution(mesh):
    return jax.shard_map(
        shards,
        mesh=mesh,
        in_specs=(
            P(("users", "ctx"), None),
            P(("users", "ctx"), None),
            P(("users", "ctx")),
            P("users", None),
            P(),
            P("users", None),
            P("users", "ctx", None),
            P("users", "ctx", None),
            P("users"),
            P("users", "ctx"),
            P(),
            P(),
        ),
        out_specs=P(("users", "ctx"), None),
        check_vma=False,
    )
```

profile of v0, /device:TPU:1, one launch (start us, length us, event | category | flops | bytes accessed | tf_op | source)
XLA Modules:
  0.0 300.3 jit_solution(16034690586346479970)
XLA Ops:
  6.5 0.7 all-gather.3.cloned.1.call-update
  7.3 2.4 broadcast_in_dim.96
  9.6 15.0 %all-to-all-start.1 = ((bf16[64,16,1024]{2,1,0:T(8,128)(2,1)}), bf16[64,16,1024]{2,1,0:T(8,128)(2,1)S(1)}, u32[]{:S(2)}, u32[]{:S(2)}) async-start(bf16[64,16,1024]{2,1,0:T(8,128)(2,1)} %broadcast_in_dim.96), calls=%async_computation.1 | async-start | bytes 4194304 | tf_op jit(solution)/shard_map/all_to_all | solution.py:14
  24.7 0.2 convert_reduce_fusion.2
  24.9 54.3 %all-to-all-done.1 = bf16[64,16,1024]{2,1,0:T(8,128)(2,1)S(1)} async-done(((bf16[64,16,1024]{2,1,0:T(8,128)(2,1)}), bf16[64,16,1024]{2,1,0:T(8,128)(2,1)S(1)}, u32[]{:S(2)}, u32[]{:S(2)}) %all-to-all-start.1) | async-done | bytes 2097184 | tf_op jit(solution)/shard_map/all_to_all | solution.py:14
  79.2 0.7 convolution_convert_fusion
  79.9 0.1 reshape.197
  80.0 21.7 %all_to_all.26 = bf16[64,2,1024]{2,1,0:T(2,128)(2,1)S(1)} all-to-all(bf16[64,2,1024]{2,1,0:T(2,128)(2,1)S(1)} %reshape.197), channel_id=1, replica_groups=mesh['users'=64,'ctx'=8] {'users'}, dimensions={0} | all-to-all | bytes 524288 | tf_op jit(solution)/shard_map/all_to_all | solution.py:92
  101.7 0.1 reshape.198
  101.8 14.6 %all-gather.3.cloned.1.call-done = bf16[1024,4096]{1,0:T(8,128)(2,1)} async-done(((bf16[16,4096]{1,0:T(8,128)(2,1)}), bf16[1024,4096]{1,0:T(8,128)(2,1)}) %all-gather.3.cloned.1.call-update) | async-done | bytes 8388624 | tf_op jit(solution)/shard_map/all_gather | solution.py:105
  116.5 4.7 %multiply_convert_fusion = bf16[128,4096]{1,0:T(8,128)(2,1)S(1)} fusion(bf16[128,1024]{1,0:T(8,128)(2,1)S(1)} %reshape.198, bf16[1024,4096]{1,0:T(8,128)(2,1)} %all-gather.3.cloned.1.call-done), kind=kOutput, calls=%fused_computation.63 | convolution fusion | flops 1076363264 | bytes 9699328 | tf_op jit(solution)/shard_map/dot_general | solution.py:106
  121.2 1.0 copy-done.1
  122.2 0.8 slice_bitcast_fusion
  123.2 0.8 convert_element_type.88
  124.0 7.0 %all-to-all-start = ((bf16[64,1,2]{2,1,0:T(2,128)(2,1)}), bf16[64,1,2]{2,1,0:T(2,128)(2,1)S(1)}, u32[]{:S(2)}, u32[]{:S(2)}) async-start(bf16[64,1,2]{2,1,0:T(2,128)(2,1)} %convert_element_type.88), calls=%async_computation | async-start | bytes 65536 | tf_op jit(solution)/shard_map/all_to_all | solution.py:99
  131.6 2.9 copy.43
  134.5 0.4 fusion.40
  134.9 2.4 copy.47
  137.3 3.9 %copy.42 = bf16[1,1024,1024]{1,2,0:T(8,128)(2,1)} copy(bf16[1,1024,1024]{2,1,0:T(8,128)(2,1)} %param.23) | data formatting | bytes 4194304 | tf_op args[7]
  141.3 0.1 maximum_reduce_fusion
  141.4 0.1 max.11
  141.5 0.1 compare_reduce_fusion
  141.7 0.1 gt.7
  141.8 0.2 fusion.44
  142.0 0.2 copy_bitcast_fusion
  142.2 18.1 %all-gather.5.cloned.1.call-done = bf16[1024,1024]{1,0:T(8,128)(2,1)} async-done(((bf16[128,1024]{1,0:T(8,128)(2,1)}), bf16[1024,1024]{1,0:T(8,128)(2,1)}) %all-gather.5.cloned.1.call-update) | async-done | bytes 2097168 | tf_op jit(solution)/shard_map/all_gather | solution.py:161
  160.3 50.7 %while.38 = (s32[]{:T(128)}, bf16[2,512,1024]{2,1,0:T(8,128)(2,1)}, pred[128]{0:T(512)(128)(4,1)S(1)}, s32[2]{0:T(128)S(1)}, bf16[2,512,1024]{2,1,0:T(8,128)(2,1...) while((s32[]{:T(128)}, bf16[2,512,1024]{2,1,0:T(8,128)(2,1)}, ...), condition=%wide.region_5.6_spmd.clone, body=%wide.region_2.5_spmd.clone.sunk | while | flops 818569728 | bytes 27956100 | solution.py:170
  160.3 0.6 dynamic_slice.60
  160.9 0.7 fusion.72
  161.6 0.1 compare_and_fusion.2
  161.7 1.3 constant_dynamic-slice_fusion.2
  163.0 0.5 copy.64
  163.6 2.5 convolution_bitcast_fusion.2
  166.1 1.9 copy.65
  168.0 1.4 copy.66
  169.3 14.6 %while.39 = (s32[]{:T(128)}, f32[512,8,128]{0,2,1:T(8,128)S(1)}, bf16[1024,8,128]{0,2,1:T(8,128)(2,1)}, pred[1024]{0:T(1024)(128)(4,1)S(1)}, bf16[1024,8,128]{2,...) while((s32[]{:T(128)}, f32[512,8,128]{0,2,1:T(8,128)S(1)}, ...), condition=%wide.region_4.4_spmd, body=%wide.region_3.3_spmd.sunk | while | flops 545783808 | bytes 6317987 | solution.py:158
  169.4 3.5 %bitcast_add_fusion.2 = f32[512,8,128]{0,2,1:T(8,128)S(1)} fusion(f32[512,8,128]{0,2,1:T(8,128)S(1)} %get-tuple-element.659, bf16[512,8,128]{2,0,1:T(8,128)(2,1)} %get-tuple-element.674, f32[8,256]{1,0:T(8,128)S(1)} %dynamic-slice_bitcast_fusion.2, pred[256]{0:T(512)(128)(4,1)S(1)} %dynamic_slice.64, bf16[1024,8,128]{2,0,1:T(8,128)(2,1)} %get-tuple-element.673, ...), kind=kOutput, calls=%fused_computation.3.clone.1 | convolution fusion | flops 545783808 | bytes 6300928 | tf_op jit(solution)/shard_map/while/body/eval_jaxpr/while/body/eval_jaxpr/hkq,khd->qhd/dot_general | solution.py:49
  173.1 3.5 %bitcast_add_fusion.2 = f32[512,8,128]{0,2,1:T(8,128)S(1)} fusion(f32[512,8,128]{0,2,1:T(8,128)S(1)} %get-tuple-element.659, bf16[512,8,128]{2,0,1:T(8,128)(2,1)} %get-tuple-element.674, f32[8,256]{1,0:T(8,128)S(1)} %dynamic-slice_bitcast_fusion.2, pred[256]{0:T(512)(128)(4,1)S(1)} %dynamic_slice.64, bf16[1024,8,128]{2,0,1:T(8,128)(2,1)} %get-tuple-element.673, ...), kind=kOutput, calls=%fused_computation.3.clone.1 | convolution fusion | flops 545783808 | bytes 6300928 | tf_op jit(solution)/shard_map/while/body/eval_jaxpr/while/body/eval_jaxpr/hkq,khd->qhd/dot_general | solution.py:49
  176.7 3.5 %bitcast_add_fusion.2 = f32[512,8,128]{0,2,1:T(8,128)S(1)} fusion(f32[512,8,128]{0,2,1:T(8,128)S(1)} %get-tuple-element.659, bf16[512,8,128]{2,0,1:T(8,128)(2,1)} %get-tuple-element.674, f32[8,256]{1,0:T(8,128)S(1)} %dynamic-slice_bitcast_fusion.2, pred[256]{0:T(512)(128)(4,1)S(1)} %dynamic_slice.64, bf16[1024,8,128]{2,0,1:T(8,128)(2,1)} %get-tuple-element.673, ...), kind=kOutput, calls=%fused_computation.3.clone.1 | convolution fusion | flops 545783808 | bytes 6300928 | tf_op jit(solution)/shard_map/while/body/eval_jaxpr/while/body/eval_jaxpr/hkq,khd->qhd/dot_general | solution.py:49
  180.4 3.5 %bitcast_add_fusion.2 = f32[512,8,128]{0,2,1:T(8,128)S(1)} fusion(f32[512,8,128]{0,2,1:T(8,128)S(1)} %get-tuple-element.659, bf16[512,8,128]{2,0,1:T(8,128)(2,1)} %get-tuple-element.674, f32[8,256]{1,0:T(8,128)S(1)} %dynamic-slice_bitcast_fusion.2, pred[256]{0:T(512)(128)(4,1)S(1)} %dynamic_slice.64, bf16[1024,8,128]{2,0,1:T(8,128)(2,1)} %get-tuple-element.673, ...), kind=kOutput, calls=%fused_computation.3.clone.1 | convolution fusion | flops 545783808 | bytes 6300928 | tf_op jit(solution)/shard_map/while/body/eval_jaxpr/while/body/eval_jaxpr/hkq,khd->qhd/dot_general | solution.py:49
  183.9 0.6 copy.67
  184.5 1.1 constant_dynamic-update-slice_fusion.2
  185.6 0.6 dynamic_slice.60
  186.2 0.7 fusion.72
  186.9 0.1 compare_and_fusion.2
  187.0 1.3 constant_dynamic-slice_fusion.2
  188.3 0.5 copy.64
  188.9 2.5 convolution_bitcast_fusion.2
  191.4 1.9 copy.65
  193.3 1.4 copy.66
  194.7 14.6 %while.39 = (s32[]{:T(128)}, f32[512,8,128]{0,2,1:T(8,128)S(1)}, bf16[1024,8,128]{0,2,1:T(8,128)(2,1)}, pred[1024]{0:T(1024)(128)(4,1)S(1)}, bf16[1024,8,128]{2,...) while((s32[]{:T(128)}, f32[512,8,128]{0,2,1:T(8,128)S(1)}, ...), condition=%wide.region_4.4_spmd, body=%wide.region_3.3_spmd.sunk | while | flops 545783808 | bytes 6317987 | solution.py:158
  194.7 3.5 %bitcast_add_fusion.2 = f32[512,8,128]{0,2,1:T(8,128)S(1)} fusion(f32[512,8,128]{0,2,1:T(8,128)S(1)} %get-tuple-element.659, bf16[512,8,128]{2,0,1:T(8,128)(2,1)} %get-tuple-element.674, f32[8,256]{1,0:T(8,128)S(1)} %dynamic-slice_bitcast_fusion.2, pred[256]{0:T(512)(128)(4,1)S(1)} %dynamic_slice.64, bf16[1024,8,128]{2,0,1:T(8,128)(2,1)} %get-tuple-element.673, ...), kind=kOutput, calls=%fused_computation.3.clone.1 | convolution fusion | flops 545783808 | bytes 6300928 | tf_op jit(solution)/shard_map/while/body/eval_jaxpr/while/body/eval_jaxpr/hkq,khd->qhd/dot_general | solution.py:49
  198.4 3.5 %bitcast_add_fusion.2 = f32[512,8,128]{0,2,1:T(8,128)S(1)} fusion(f32[512,8,128]{0,2,1:T(8,128)S(1)} %get-tuple-element.659, bf16[512,8,128]{2,0,1:T(8,128)(2,1)} %get-tuple-element.674, f32[8,256]{1,0:T(8,128)S(1)} %dynamic-slice_bitcast_fusion.2, pred[256]{0:T(512)(128)(4,1)S(1)} %dynamic_slice.64, bf16[1024,8,128]{2,0,1:T(8,128)(2,1)} %get-tuple-element.673, ...), kind=kOutput, calls=%fused_computation.3.clone.1 | convolution fusion | flops 545783808 | bytes 6300928 | tf_op jit(solution)/shard_map/while/body/eval_jaxpr/while/body/eval_jaxpr/hkq,khd->qhd/dot_general | solution.py:49
  202.1 3.5 %bitcast_add_fusion.2 = f32[512,8,128]{0,2,1:T(8,128)S(1)} fusion(f32[512,8,128]{0,2,1:T(8,128)S(1)} %get-tuple-element.659, bf16[512,8,128]{2,0,1:T(8,128)(2,1)} %get-tuple-element.674, f32[8,256]{1,0:T(8,128)S(1)} %dynamic-slice_bitcast_fusion.2, pred[256]{0:T(512)(128)(4,1)S(1)} %dynamic_slice.64, bf16[1024,8,128]{2,0,1:T(8,128)(2,1)} %get-tuple-element.673, ...), kind=kOutput, calls=%fused_computation.3.clone.1 | convolution fusion | flops 545783808 | bytes 6300928 | tf_op jit(solution)/shard_map/while/body/eval_jaxpr/while/body/eval_jaxpr/hkq,khd->qhd/dot_general | solution.py:49
  205.7 3.5 %bitcast_add_fusion.2 = f32[512,8,128]{0,2,1:T(8,128)S(1)} fusion(f32[512,8,128]{0,2,1:T(8,128)S(1)} %get-tuple-element.659, bf16[512,8,128]{2,0,1:T(8,128)(2,1)} %get-tuple-element.674, f32[8,256]{1,0:T(8,128)S(1)} %dynamic-slice_bitcast_fusion.2, pred[256]{0:T(512)(128)(4,1)S(1)} %dynamic_slice.64, bf16[1024,8,128]{2,0,1:T(8,128)(2,1)} %get-tuple-element.673, ...), kind=kOutput, calls=%fused_computation.3.clone.1 | convolution fusion | flops 545783808 | bytes 6300928 | tf_op jit(solution)/shard_map/while/body/eval_jaxpr/while/body/eval_jaxpr/hkq,khd->qhd/dot_general | solution.py:49
  209.3 0.6 copy.67
  209.9 1.1 constant_dynamic-update-slice_fusion.2
  211.0 49.5 %all_to_all.27 = bf16[8,128,1024]{2,1,0:T(8,128)(2,1)S(1)} all-to-all(bf16[8,128,1024]{2,1,0:T(8,128)(2,1)} %bitcast.87), channel_id=1, replica_groups=mesh['users'=64,'ctx'=8] {'ctx'}, dimensions={0} | all-to-all | bytes 4194304 | tf_op jit(solution)/shard_map/all_to_all | solution.py:35
  260.5 0.5 convert_reduce_fusion
  261.0 0.2 multiply_reduce_fusion
  261.2 1.1 multiply_convert_fusion.1
  262.3 0.1 reshape.202
  262.5 30.0 %all_to_all.28 = bf16[64,2,1024]{2,1,0:T(2,128)(2,1)S(1)} all-to-all(bf16[64,2,1024]{2,1,0:T(2,128)(2,1)S(1)} %reshape.202), channel_id=1, replica_groups=mesh['users'=64,'ctx'=8] {'users'}, dimensions={0} | all-to-all | bytes 524288 | tf_op jit(solution)/shard_map/all_to_all | solution.py:177
  292.6 0.9 convolution_convert_fusion.1
  (60 shorter events, 1.1 us)
Async XLA Ops:
  6.5 127.9 %copy-start = (f32[32,8]{0,1:T(8,128)S(1)}, f32[32,8]{0,1:T(8,128)}, u32[]{:S(2)}) copy-start(f32[32,8]{0,1:T(8,128)} %param.26) | copy-start | bytes 3076
  6.5 109.9 %all-gather.3.cloned.1.call-start = ((), (), s32[]{:S(2)}) async-start(), calls=%async_computation.5 | async-start | bytes 8519680 | tf_op jit(solution)/shard_map/all_gather | solution.py:105
  9.6 15.0 %copy-start.10 = (s32[64,1]{0,1:T(1,128)S(1)}, s32[64,1]{0,1:T(1,128)}, u32[]{:S(2)}) copy-start(s32[64,1]{0,1:T(1,128)} %param.17) | copy-start | bytes 772
  9.6 69.6 %copy-start.4 = (bf16[64,1024]{1,0:T(8,128)(2,1)S(1)}, bf16[64,1024]{1,0:T(8,128)(2,1)}, u32[]{:S(2)}) copy-start(bf16[64,1024]{1,0:T(8,128)(2,1)} %param.16) | copy-start | bytes 393220
  9.6 69.6 %copy-start.5 = (f32[1024]{0:T(1024)S(1)}, f32[1024]{0:T(1024)}, u32[]{:S(2)}) copy-start(f32[1024]{0:T(1024)} %param.20) | copy-start | bytes 12292
  9.6 69.6 %all-to-all-start.1 = ((bf16[64,16,1024]{2,1,0:T(8,128)(2,1)}), bf16[64,16,1024]{2,1,0:T(8,128)(2,1)S(1)}, u32[]{:S(2)}, u32[]{:S(2)}) async-start(bf16[64,16,1024]{2,1,0:T(8,128)(2,1)} %broadcast_in_dim.96), calls=%async_computation.1 | async-start | bytes 4194304 | tf_op jit(solution)/shard_map/all_to_all | solution.py:14
  24.6 135.7 %all-gather.5.cloned.1.call-start = ((), (), s32[]{:S(2)}) async-start(), calls=%async_computation.6 | async-start | bytes 2359296 | tf_op jit(solution)/shard_map/all_gather | solution.py:161
  24.9 98.2 %copy-start.7 = (s32[64]{0:T(128)}, s32[64]{0:T(128)S(1)}, u32[]{:S(2)}) copy-start(s32[64]{0:T(128)S(1)} %multiply_add_fusion) | copy-start | bytes 772
  101.8 21.2 %copy-start.11 = (s32[64]{0:T(128)S(1)}, s32[64]{0:T(128)}, u32[]{:S(2)}) copy-start(s32[64]{0:T(128)} %param.18) | copy-start | bytes 772
  121.2 1.0 copy-start.1
  124.0 17.3 %all-to-all-start = ((bf16[64,1,2]{2,1,0:T(2,128)(2,1)}), bf16[64,1,2]{2,1,0:T(2,128)(2,1)S(1)}, u32[]{:S(2)}, u32[]{:S(2)}) async-start(bf16[64,1,2]{2,1,0:T(2,128)(2,1)} %convert_element_type.88), calls=%async_computation | async-start | bytes 65536 | tf_op jit(solution)/shard_map/all_to_all | solution.py:99
  131.6 2.9 copy-start.9
  160.3 3.3 %copy-start.2 = (bf16[128,8,128]{2,0,1:T(8,128)(2,1)}, bf16[128,8,128]{2,0,1:T(8,128)(2,1)S(1)}, u32[]{:S(2)}) copy-start(bf16[128,8,128]{2,0,1:T(8,128)(2,1)S(1)} %get-tuple-element.723) | copy-start | bytes 786436 | tf_op jit(solution)/shard_map/while
  184.5 1.1 copy-start.3
  185.6 3.3 %copy-start.2 = (bf16[128,8,128]{2,0,1:T(8,128)(2,1)}, bf16[128,8,128]{2,0,1:T(8,128)(2,1)S(1)}, u32[]{:S(2)}) copy-start(bf16[128,8,128]{2,0,1:T(8,128)(2,1)S(1)} %get-tuple-element.723) | copy-start | bytes 786436 | tf_op jit(solution)/shard_map/while
  209.9 1.1 copy-start.3
  260.5 0.7 copy-start.6
  261.0 31.6 %copy-start.8 = (s32[64]{0:T(128)S(1)}, s32[64]{0:T(128)}, u32[]{:S(2)}) copy-start(s32[64]{0:T(128)} %copy-done.7) | copy-start | bytes 772
Sparse Core Ops, SparseCore 0:
  10.7 105.7 all-gather.2
  123.1 37.1 all-gather.4
where the time goes:
time: 301 us; the launch traced here: 300 us
  blocking collectives  101 us (34%)
  waiting for transfers between devices  87.8 us (29%)
  matrix products  40.1 us (13%)
  local copies, waits for them, and re-layouts  30.5 us (10%)
  starting transfers between devices  22 us (7%)
  between operations  14.3 us (5%)
  other arithmetic  4.04 us (1%)
    all_to_all x1, waiting for transfers between devices, from_everyone(): return lax.all_to_all(copies, axis, split_axis=0, concat_axis=0, tiled=True)  54.3 us
    all_to_all x1, blocking collectives, summed_on_arrival(): lax.all_to_all(parts, axis, split_axis=0, concat_axis=0, tiled=True)  49.5 us
    dot_general x10, matrix products, weighted_sum(): jnp.einsum('hkq,khd->qhd', weights, values_part, preferred_element_type=j...  33.2 us
    all_to_all x1, blocking collectives, shards(): lax.all_to_all(gated.reshape(owner_count, capacity, feature_width), 'user...  30 us
    all_to_all x1, blocking collectives, shards(): lax.all_to_all(outgoing.reshape(owner_count, capacity, feature_width), 'u...  21.7 us
    all_gather x1, waiting for transfers between devices, shards(): query_piece = lax.all_gather(new_queries, 'ctx', axis=0, tiled=True)  18.1 us
    all_to_all x1, starting transfers between devices, from_everyone(): return lax.all_to_all(copies, axis, split_axis=0, concat_axis=0, tiled=True)  15 us
    all_gather x1, waiting for transfers between devices, shards(): project_full = lax.all_gather(project_weight, 'users', axis=0, tiled=True)  14.6 us
  transfers between devices with their start and end apart: 4, of which 3 were waited for; matrix products, arithmetic and copies ran while one was open for 5% of the time, Pallas kernels for 0%

commit v1 on v0

v1 whole, which is shorter than its diff:
```python
import jax
import jax.numpy as jnp
from jax import lax
from jax.experimental import pallas as pl
from jax.experimental.pallas import tpu as pltpu
from jax.sharding import PartitionSpec as P

MESH = pl.DeviceIdType.MESH
F32, BF16, I32 = jnp.float32, jnp.bfloat16, jnp.int32

NX = 4
XC = 8
NZ = 8
NY = 8
ROWS = 64
SLOTS = 128
D = 1024
DL = D + 128
CACHE = 1024
HEADS = 8
HW = 128
BUCKETS = 32
EPS = 1e-05
BEGINS = (None, 2048, 3072, 1024, 0)


def half_silu(v):
    return v + v * jnp.tanh(v)


def kernel(
    ev, own_col, own_row, buck_row, wcs, wps, cbias, ck, cv, clen, cbuck, tbt, gain,
    out,
    wbuf, kb, kt, vb, s1, r1, s2, r2, s3, r3, s4, r4, qb, part, ss, rr, newk, newv, gates, cbh, nbh, mask,
    kv_sem, xs, xr, zs, zr, ps, pr, ys, yr, rss, rsr, ts, tr,
):
    u, c = lax.axis_index("users"), lax.axis_index("ctx")
    z, xc = lax.div(u, XC), lax.rem(u, XC)
    x, k = lax.div(xc, 2), lax.rem(xc, 2)
    c_up, c_down = lax.rem(c + 1, NY), lax.rem(c + NY - 1, NY)

    def dev(z_, x_, k_):
        return (z_ * XC + x_ * 2 + k_, c)

    def remote(src, dst, send, recv, to):
        return pltpu.make_async_remote_copy(
            src_ref=src, dst_ref=dst, send_sem=send, recv_sem=recv, device_id=to, device_id_type=MESH
        )

    def xcopy(m, i):
        ref = wbuf.at[m, z, x, k]
        return remote(ref, ref, xs.at[m, i - 1], xr.at[m, i - 1], dev(z, lax.rem(x + i, NX), k))

    def zcopy(m, way, s, h):
        zz = lax.rem(z - s + NZ, NZ) if way == 0 else lax.rem(z + s, NZ)
        to = lax.rem(z + 1, NZ) if way == 0 else lax.rem(z + NZ - 1, NZ)
        i = 2 * s + h if s < 3 else 6
        ref = wbuf.at[m, zz, pl.ds(2 * h, 2), k]
        return remote(ref, ref, zs.at[m, way, i], zr.at[m, way, i], dev(to, x, k))

    def pcopy(m, j):
        ref = wbuf.at[m, lax.rem(z + j, NZ), :, k]
        return remote(ref, ref, ps.at[m, j], pr.at[m, j], dev(z, x, 1 - k))

    def x_start(m):
        for i in range(1, NX):
            xcopy(m, i).start()

    def ring_begin(m):
        for i in range(1, NX):
            xcopy(m, i).wait_recv()
        for h in range(2):
            for way in range(2):
                zcopy(m, way, 0, h).start()
        pcopy(m, 0).start()

    def ring_step(m, s):
        for h in range(2):
            for way in range(2):
                if s == 3 and h != way:
                    continue
                zcopy(m, way, s, h).wait_recv()
                if s < 2 or (s == 2 and h == way):
                    zcopy(m, way, s + 1, h).start()
        if s < 3:
            pcopy(m, 7 - s).start()
            pcopy(m, 1 + s).start()
        else:
            pcopy(m, 4).start()

    def ring_end(m):
        for j in range(NZ):
            pcopy(m, j).wait_recv()

    def gather_sent(m):
        for i in range(1, NX):
            xcopy(m, i).wait_send()
        for way in range(2):
            for s in range(4):
                for h in range(2):
                    if s < 3 or h == way:
                        zcopy(m, way, s, h).wait_send()
        for j in range(NZ):
            pcopy(m, j).wait_send()

    def tcopy(leg, i):
        src, dst = ((s1, r1), (s2, r2), (s3, r3), (s4, r4))[leg]
        if leg in (0, 3):
            to = lax.rem(z + i, NZ)
            return remote(src.at[to], dst.at[z], ts.at[leg, i - 1], tr.at[leg, i - 1], dev(to, x, k))
        to = lax.rem(xc + i, XC)
        return remote(src.at[to], dst.at[xc], ts.at[leg, i - 1], tr.at[leg, i - 1], (z * XC + to, c))

    def t_start(leg):
        for i in range(1, 8):
            tcopy(leg, i).start()
        src, dst = ((s1, r1), (s2, r2), (s3, r3), (s4, r4))[leg]
        mine = z if leg in (0, 3) else xc
        dst[mine] = src[mine]

    def t_wait(leg):
        for i in range(1, 8):
            tcopy(leg, i).wait_recv()

    def ycopy(way, e, h):
        si, di, to = (e, e + 1, c_up) if way == 0 else ((8 - e) % 8, 7 - e, c_down)
        i = 2 * e + h if e < 3 else 6
        return remote(qb.at[si, h], qb.at[di, h], ys.at[way, i], yr.at[way, i], (u, to))

    def y_stage(s):
        for h in range(2):
            for way in range(2):
                if s == 3 and h != way:
                    continue
                ycopy(way, s, h).wait_recv()
                if s < 2 or (s == 2 and h == way):
                    ycopy(way, s + 1, h).start()

    def scopy(way, d, h):
        to = c_down if way == 0 else c_up
        i = 2 * (d - 1) + h if d < 4 else 6
        return remote(ss.at[way, d - 1, h], rr.at[way, d - 1, h], rss.at[way, i], rsr.at[way, i], (u, to))

    def rs_send(way, d, h):
        v = part[d if way == 0 else 8 - d, h]
        if d < 3 or (d == 3 and h == way):
            scopy(way, d + 1, h).wait_recv()
            v = v + rr[way, d, h].astype(F32)
        ss[way, d - 1, h] = v.astype(BF16)
        scopy(way, d, h).start()

    for m in range(5):
        wbuf[m, z, x, k] = wcs[...] if m == 0 else wps[:, BEGINS[m] : BEGINS[m] + D]
    k_in = pltpu.make_async_copy(ck.at[0], kb, kv_sem.at[0])
    v_in = pltpu.make_async_copy(cv.at[0], vb, kv_sem.at[1])
    k_in.start()
    v_in.start()

    barrier = pltpu.get_barrier_semaphore()
    peers = [dev(lax.rem(z + i, NZ), x, k) for i in range(1, NZ)]
    peers += [(z * XC + lax.rem(xc + i, XC), c) for i in range(1, XC)]
    peers += [(u, c_up), (u, c_down)]
    for peer in peers:
        pl.semaphore_signal(barrier, inc=1, device_id=peer, device_id_type=MESH)
    pl.semaphore_wait(barrier, len(peers))

    x_start(0)
    x_start(1)

    oc, orow = own_col[...], own_row[...]
    first = lax.broadcasted_iota(I32, (ROWS, ROWS), 0)
    second = lax.broadcasted_iota(I32, (ROWS, ROWS), 1)
    same = oc == orow
    rank_row = jnp.sum(jnp.where(same & (first < second), 1.0, 0.0), axis=0, keepdims=True)
    slot_row = orow * 2 + rank_row.astype(I32)
    placing = lax.broadcasted_iota(I32, (SLOTS, ROWS), 0) == slot_row
    place = jnp.where(placing, 1.0, 0.0).astype(BF16)
    label = jnp.sum(jnp.where(placing, buck_row[...].astype(F32), 0.0), axis=1, keepdims=True)
    label_block = jnp.broadcast_to(label, (SLOTS, HW)).astype(BF16)
    s1[:, :, D:] = label_block.reshape(NZ, 16, HW)

    to_slot = lax.broadcasted_iota(I32, (SLOTS, SLOTS), 0)
    from_slot = lax.broadcasted_iota(I32, (SLOTS, SLOTS), 1)
    swapped = ((to_slot >> 1) & 7) * 16 + (to_slot >> 4) * 2 + (to_slot & 1)
    swap = jnp.where(swapped == from_slot, 1.0, 0.0).astype(BF16)

    ring_begin(0)

    level = lax.broadcasted_iota(I32, (BUCKETS, CACHE), 0)
    picked = jnp.where(level == cbuck[...], 1.0, 0.0)
    cbh[...] = 0.5 * jnp.dot(tbt[...], picked, precision=lax.Precision.HIGHEST, preferred_element_type=F32)
    k_in.wait()

    def turn(h, _):
        lanes = pl.ds(pl.multiple_of(h * HW, HW), HW)
        kt[lanes, :] = kb[:, lanes].T
        return _

    lax.fori_loop(0, 3, turn, 0)
    ring_step(0, 0)
    lax.fori_loop(3, 6, turn, 0)
    ring_step(0, 1)
    lax.fori_loop(6, 8, turn, 0)
    v_in.wait()
    live = clen[0] - c * CACHE

    def blank(i, _):
        rows = pl.ds(pl.multiple_of(i * 128, 128), 128)
        at = i * 128 + lax.broadcasted_iota(I32, (128, D), 0)
        vb[rows, :] = jnp.where(at < live, vb[rows, :].astype(F32), 0.0).astype(BF16)
        return _

    ring_step(0, 2)
    ring_begin(1)
    lax.fori_loop(0, CACHE // 128, blank, 0)
    ring_step(0, 3)
    ring_end(0)

    def times(rows_value, m, n):
        block = wbuf[m, :, :, :, :, n * 256 : (n + 1) * 256].reshape(D, 256)
        return jnp.dot(rows_value, block, preferred_element_type=F32)

    event_rows = ev[...]
    for n in range(4):
        cols = slice(n * 256, (n + 1) * 256)
        source = event_rows[:, cols].astype(F32)
        crossed = (source * (times(event_rows, 0, n) + cbias[:, cols]) + source).astype(BF16)
        placed = jnp.dot(place, crossed, preferred_element_type=F32).astype(BF16)
        s1[:, :, cols] = placed.reshape(NZ, 16, 256)
    t_start(0)
    x_start(2)
    ring_step(1, 0)
    t_wait(0)
    moved = jnp.dot(swap, r1[...].reshape(SLOTS, DL), preferred_element_type=F32)
    s2[...] = moved.astype(BF16).reshape(XC, 16, DL)
    t_start(1)
    ring_step(1, 1)
    ring_step(1, 2)
    ring_begin(2)
    ring_step(1, 3)
    x_start(3)
    x_start(4)
    t_wait(1)
    ring_end(1)

    arrived = r2[:, :, :D].reshape(SLOTS, D)

    def projected(m, n):
        return half_silu(0.5 * times(arrived, m, n))

    for n in range(4):
        qb[0, n // 2, :, (n % 2) * 256 : (n % 2 + 1) * 256] = projected(1, n).astype(BF16)
        if n % 2:
            ycopy(0, 0, n // 2).start()
            ycopy(1, 0, n // 2).start()

    labels = r2[:, :, D:].reshape(SLOTS, HW).astype(F32).T[:BUCKETS]
    new_picked = jnp.where(labels == lax.broadcasted_iota(I32, (BUCKETS, SLOTS), 0).astype(F32), 1.0, 0.0)
    nbh[...] = 0.5 * jnp.dot(tbt[...], new_picked, precision=lax.Precision.HIGHEST, preferred_element_type=F32)

    half_scale = 0.5 * HW ** (-0.5)

    def attend(blocks, half):
        def one_head(i, _):
            h = half * 4 + i
            lanes = pl.ds(pl.multiple_of(i * HW, HW), HW)
            wide = pl.ds(pl.multiple_of(h * HW, HW), HW)
            q = jnp.concatenate([qb[d, half, :, lanes] for d in blocks], axis=0)
            s = jnp.dot(q, kt[wide, :], preferred_element_type=F32)
            s = s * half_scale + cbh[pl.ds(h, 1), :]
            w = half_silu(s).astype(BF16)
            o = jnp.dot(w, vb[:, wide], preferred_element_type=F32)
            for j, d in enumerate(blocks):
                part[d, half, :, lanes] = o[j * SLOTS : (j + 1) * SLOTS]
            return _

        lax.fori_loop(0, 4, one_head, 0)

    def shard_of(slot):
        return ((slot >> 1) & 7) * XC + (slot >> 4)

    key_order = (shard_of(from_slot) * NY + c) * 2 + (from_slot & 1)
    for d in range(NY):
        origin = lax.rem(c - d + NY, NY)
        query_order = (shard_of(to_slot) * NY + origin) * 2 + (to_slot & 1)
        mask[d] = jnp.where(key_order <= query_order, 1.0, 0.0)

    def attend_new(begin, end):
        count = end - begin

        def one_head(h, _):
            half = lax.div(h, 4)
            lanes = pl.ds(pl.multiple_of(lax.rem(h, 4) * HW, HW), HW)
            wide = pl.ds(pl.multiple_of(h * HW, HW), HW)
            q = qb[begin:end, half, :, lanes].reshape(count * SLOTS, HW)
            s = lax.dot_general(q, newk[:, wide], (((1,), (1,)), ((), ())), preferred_element_type=F32)
            s = s * half_scale + nbh[pl.ds(h, 1), :]
            w = (half_silu(s) * mask[begin:end].reshape(count * SLOTS, SLOTS)).astype(BF16)
            o = jnp.dot(w, newv[:, wide], preferred_element_type=F32)
            part[begin:end, half, :, lanes] += o.reshape(count, SLOTS, HW)
            return _

        lax.fori_loop(0, HEADS, one_head, 0)

    attend((0,), 0)
    ring_step(2, 0)
    attend((0,), 1)
    y_stage(0)
    ring_step(2, 1)
    attend((1, 7), 0)
    ring_step(2, 2)
    ring_begin(3)
    ring_step(2, 3)
    attend((1, 7), 1)
    ring_end(2)
    y_stage(1)
    for n in range(4):
        newk[:, n * 256 : (n + 1) * 256] = projected(2, n).astype(BF16)
    ring_step(3, 0)
    attend((2, 6), 0)
    ring_step(3, 1)
    attend((2, 6), 1)
    y_stage(2)
    ring_step(3, 2)
    ring_begin(4)
    attend((3, 5), 0)
    ring_step(3, 3)
    attend((3, 5), 1)
    ring_end(3)
    for n in range(4):
        newv[:, n * 256 : (n + 1) * 256] = projected(3, n).astype(BF16)
    attend_new(5, 8)
    attend_new(0, 4)
    rs_send(0, 3, 1)
    rs_send(1, 3, 0)
    y_stage(3)
    attend((4,), 0)
    attend((4,), 1)
    attend_new(4, 5)
    rs_send(0, 4, 0)
    rs_send(1, 4, 1)
    ring_step(4, 0)
    rs_send(0, 3, 0)
    rs_send(1, 3, 1)
    ring_step(4, 1)
    for h in range(2):
        rs_send(0, 2, 1 - h)
        rs_send(1, 2, h)
    ring_step(4, 2)
    ring_step(4, 3)
    ring_end(4)
    for n in range(4):
        gates[:, n * 256 : (n + 1) * 256] = projected(4, n).astype(BF16)
    for h in range(2):
        rs_send(0, 1, 1 - h)
        rs_send(1, 1, h)

    for h in range(2):
        for way in range(2):
            scopy(way, 1, h).wait_recv()
    attended = [part[0, h] + rr[0, 0, h].astype(F32) + rr[1, 0, h].astype(F32) for h in range(2)]
    total = jnp.sum(attended[0], axis=1, keepdims=True) + jnp.sum(attended[1], axis=1, keepdims=True)
    centered = [v - total / D for v in attended]
    squares = sum(jnp.sum(v * v, axis=1, keepdims=True) for v in centered)
    inverse = lax.rsqrt(squares / D + EPS)
    for h in range(2):
        cols = slice(h * 512, (h + 1) * 512)
        gated = centered[h] * inverse * gain[:, cols] * gates[:, cols].astype(F32)
        s3[:, :, cols] = gated.astype(BF16).reshape(XC, 16, 512)

    t_start(2)
    t_wait(2)
    moved_back = jnp.dot(swap, r3[...].reshape(SLOTS, D), preferred_element_type=F32)
    s4[...] = moved_back.astype(BF16).reshape(NZ, 16, D)
    t_start(3)
    rank_col = jnp.sum(jnp.where((own_col[...] == own_row[...]) & (second < first), 1.0, 0.0), axis=1, keepdims=True)
    slot_col = own_col[...] * 2 + rank_col.astype(I32)
    unplace = jnp.where(lax.broadcasted_iota(I32, (ROWS, SLOTS), 1) == slot_col, 1.0, 0.0).astype(BF16)
    for m in range(5):
        gather_sent(m)
    for way in range(2):
        for e in range(4):
            for h in range(2):
                if e < 3 or h == way:
                    ycopy(way, e, h).wait_send()
                    scopy(way, e + 1, h).wait_send()
    for leg in range(3):
        for i in range(1, 8):
            tcopy(leg, i).wait_send()
    t_wait(3)
    out[...] = jnp.dot(unplace, r4[...].reshape(SLOTS, D), preferred_element_type=F32).astype(BF16)
    for i in range(1, 8):
        tcopy(3, i).wait_send()


def shards(
    events, owner_id, event_bucket, cross_weight, cross_bias, project_weight,
    cache_keys, cache_values, cache_length, cache_bucket, time_bias, norm_gain,
):
    vmem = pl.BlockSpec(memory_space=pltpu.VMEM)
    whole = pl.BlockSpec(memory_space=pl.ANY)
    smem = pl.BlockSpec(memory_space=pltpu.SMEM)
    dma = pltpu.SemaphoreType.DMA
    return pl.pallas_call(
        kernel,
        out_shape=jax.ShapeDtypeStruct((ROWS, D), BF16),
        in_specs=[vmem] * 7 + [whole] * 2 + [smem] + [vmem] * 3,
        out_specs=vmem,
        scratch_shapes=[
            pltpu.VMEM((5, NZ, NX, 2, 16, D), BF16),
            pltpu.VMEM((CACHE, D), BF16),
            pltpu.VMEM((D, CACHE), BF16),
            pltpu.VMEM((CACHE, D), BF16),
            pltpu.VMEM((NZ, 16, DL), BF16),
            pltpu.VMEM((NZ, 16, DL), BF16),
            pltpu.VMEM((XC, 16, DL), BF16),
            pltpu.VMEM((XC, 16, DL), BF16),
            pltpu.VMEM((XC, 16, D), BF16),
            pltpu.VMEM((XC, 16, D), BF16),
            pltpu.VMEM((NZ, 16, D), BF16),
            pltpu.VMEM((NZ, 16, D), BF16),
            pltpu.VMEM((NY, 2, SLOTS, 512), BF16),
            pltpu.VMEM((NY, 2, SLOTS, 512), F32),
            pltpu.VMEM((2, 4, 2, SLOTS, 512), BF16),
            pltpu.VMEM((2, 4, 2, SLOTS, 512), BF16),
            pltpu.VMEM((SLOTS, D), BF16),
            pltpu.VMEM((SLOTS, D), BF16),
            pltpu.VMEM((SLOTS, D), BF16),
            pltpu.VMEM((HEADS, CACHE), F32),
            pltpu.VMEM((HEADS, SLOTS), F32),
            pltpu.VMEM((NY, SLOTS, SLOTS), F32),
            dma((2,)),
            dma((5, 3)),
            dma((5, 3)),
            dma((5, 2, 7)),
            dma((5, 2, 7)),
            dma((5, 8)),
            dma((5, 8)),
            dma((2, 7)),
            dma((2, 7)),
            dma((2, 7)),
            dma((2, 7)),
            dma((4, 7)),
            dma((4, 7)),
        ],
        compiler_params=pltpu.CompilerParams(
            collective_id=0, has_side_effects=True, vmem_limit_bytes=48 * 1024 * 1024
        ),
        name="ingest",
    )(
        events,
        owner_id,
        owner_id.reshape(1, ROWS),
        event_bucket.reshape(1, ROWS),
        cross_weight,
        project_weight,
        cross_bias.reshape(1, D),
        cache_keys,
        cache_values,
        cache_length,
        cache_bucket,
        time_bias.T,
        norm_gain.reshape(1, D),
    )


def solution(mesh):
    return jax.shard_map(
        shards,
        mesh=mesh,
        in_specs=(
            P(("users", "ctx"), None),
            P(("users", "ctx"), None),
            P(("users", "ctx")),
            P("users", None),
            P(),
            P("users", None),
            P("users", "ctx", None),
            P("users", "ctx", None),
            P("users"),
            P("users", "ctx"),
            P(),
            P(),
        ),
        out_specs=P(("users", "ctx"), None),
        check_vma=False,
    )
```

time: 301 us -> 159 us (0.53)
  Pallas kernels: 0 us -> 145 us
  blocking collectives: 101 us -> 0 us
  waiting for transfers between devices: 87.8 us -> 0 us
  matrix products: 40.1 us -> 0 us
  starting transfers between devices: 22 us -> 0 us
  local copies, waits for them, and re-layouts: 30.5 us -> 11.2 us
  between operations: 14.3 us -> 0.67 us
  other arithmetic: 4.04 us -> 0 us
    pallas_call x0 -> x1, Pallas kernels: none -> 145 us  [shards(): pl.pallas_call(kernel, out_shape=jax.ShapeDtypeStruct((ROWS, D), BF16), i...]
    all_to_all x3 -> x0, blocking collectives: 101 us -> none  [the longest x1 49.5 us: summed_on_arrival(): lax.all_to_all(parts, axis, split_axis=0, concat_axis=0, tiled=True)]
    all_to_all x2 -> x0, waiting for transfers between devices: 54.3 us -> none  [the longest x1 54.3 us: from_everyone(): return lax.all_to_all(copies, axis, split_axis=0, concat_axis=0, tiled=True)]
    dot_general x15 -> x0, matrix products: 40.1 us -> none  [the longest x10 33.2 us: weighted_sum(): jnp.einsum('hkq,khd->qhd', weights, values_part, preferred_element_type=j...]
    all_gather x2 -> x0, waiting for transfers between devices: 32.7 us -> none  [the longest x1 18.1 us: shards(): query_piece = lax.all_gather(new_queries, 'ctx', axis=0, tiled=True)]
    all_to_all x2 -> x0, starting transfers between devices: 21.9 us -> none  [the longest x1 15 us: from_everyone(): return lax.all_to_all(copies, axis, split_axis=0, concat_axis=0, tiled=True)]
    while x12 -> x0, local copies, waits for them, and re-layouts: 6.56 us -> none  [the longest x4 6.54 us: attend_block(): summed = lax.fori_loop(0, block_total, add_block, summed)]
    dynamic_slice x14 -> x0, local copies, waits for them, and re-layouts: 5.51 us -> none  [the longest x6 4.88 us: shards(): outputs = lax.map(one_block, (stacked, block_starts))]
  transfers between devices with their start and end apart: 4 -> 0, of which waited for: 3 -> 0; matrix products, arithmetic and copies ran while one was open for 5% -> 0% of each run, Pallas kernels for 0% -> 0%
where the time goes in v1:
time: 159 us; the launch traced here: 157 us
  Pallas kernels  145 us (91%)
  local copies, waits for them, and re-layouts  11.2 us (7%)
    pallas_call x1, Pallas kernels, shards(): pl.pallas_call(kernel, out_shape=jax.ShapeDtypeStruct((ROWS, D), BF16), i...  145 us
    unnamed x24, local copies, waits for them, and re-layouts  11.2 us

profile of v1, /device:TPU:1, one launch (start us, length us, event | category | flops | bytes accessed | tf_op | source)
XLA Modules:
  0.0 156.5 jit_solution(7835210255694265222)
XLA Ops:
  0.7 0.7 copy.13.own_col
  1.4 0.0 copy-start
  1.4 1.6 %copy-done = bf16[1,1024,1024]{2,1,0:T(8,128)(2,1)S(1)} copy-done((bf16[1,1024,1024]{2,1,0:T(8,128)(2,1)S(1)}, bf16[1,1024,1024]{2,1,0:T(8,128)(2,1)}, u32[]{:S(2)}) %copy-start) | copy-done | bytes 2097176
  3.0 0.0 copy-start.1
  3.0 1.6 %copy-done.1 = bf16[1,1024,1024]{2,1,0:T(8,128)(2,1)S(1)} copy-done((bf16[1,1024,1024]{2,1,0:T(8,128)(2,1)S(1)}, bf16[1,1024,1024]{2,1,0:T(8,128)(2,1)}, u32[]{:S(2)}) %copy-start.1) | copy-done | bytes 2097176
  4.6 0.0 copy-start.2
  4.6 0.9 copy-done.2
  5.5 0.0 copy-start.3
  5.5 0.9 copy-done.3
  6.4 0.0 copy-start.4
  6.4 0.8 copy-done.4
  7.2 0.0 copy-start.5
  7.2 0.7 copy-done.5
  7.8 0.0 copy-start.6
  7.8 0.7 copy-done.6
  8.5 0.0 copy-start.7
  8.5 0.7 copy-done.7
  9.2 0.0 copy-start.8
  9.2 0.7 copy-done.8
  9.9 0.0 copy-start.9
  9.9 0.7 copy-done.9
  10.6 0.0 copy-start.10
  10.6 0.7 copy-done.10
  11.2 144.7 %ingest.1 = bf16[64,1024]{1,0:T(8,128)(2,1)S(1)} custom-call(bf16[64,1024]{1,0:T(8,128)(2,1)S(1)} %copy-done.2, s32[64,1]{1,0:T(8,128)S(1)} %copy.13.own_col, s32[1,64]{1,0:T(1,128)S(1)} %bitcast.8, s32[1,64]{1,0:T(1,128)S(1)} %bitcast.9, bf16[16,1024]{1,0:T(8,128)(2,1)S(1)} %copy-done.4, bf16[16,4096]{1,0:T(8,128)(2,1)S(1)} %copy-done.3, ...), custom_call_target="tpu_custom_call" | custom-call | tf_op jit(solution)/shard_map/ingest/pallas_call | solution.py:404
  155.9 0.7 copy.16
Async XLA Ops:
  1.4 1.6 %copy-start = (bf16[1,1024,1024]{2,1,0:T(8,128)(2,1)S(1)}, bf16[1,1024,1024]{2,1,0:T(8,128)(2,1)}, u32[]{:S(2)}) copy-start(bf16[1,1024,1024]{2,1,0:T(8,128)(2,1)} %ck.1) | copy-start | bytes 6291460
  3.0 1.6 %copy-start.1 = (bf16[1,1024,1024]{2,1,0:T(8,128)(2,1)S(1)}, bf16[1,1024,1024]{2,1,0:T(8,128)(2,1)}, u32[]{:S(2)}) copy-start(bf16[1,1024,1024]{2,1,0:T(8,128)(2,1)} %cv.1) | copy-start | bytes 6291460
  4.6 0.9 copy-start.2
  5.5 0.9 copy-start.3
  6.4 0.8 copy-start.4
  7.2 0.7 copy-start.5
  7.8 0.7 copy-start.6
  8.5 0.7 copy-start.7
  9.2 0.7 copy-start.8
  9.9 0.7 copy-start.9
  10.6 0.7 copy-start.10

commit v2 on v1

--- a/solution.py
+++ b/solution.py
@@ -21,6 +21,8 @@
 HW = 128
 BUCKETS = 32
 EPS = 1e-05
+XF = 384
+VMEM_BYTES = 60 * 1024 * 1024
 BEGINS = (None, 2048, 3072, 1024, 0)
 
 
@@ -29,10 +31,10 @@
 
 
 def kernel(
-    ev, own_col, own_row, buck_row, wcs, wps, cbias, ck, cv, clen, cbuck, tbt, gain,
+    events, owners, buckets, wcs, wps, cross_bias, ck, cv, length, cache_bucket, time_bias, norm_gain,
     out,
-    wbuf, kb, kt, vb, s1, r1, s2, r2, s3, r3, s4, r4, qb, part, ss, rr, newk, newv, gates, cbh, nbh, mask,
-    kv_sem, xs, xr, zs, zr, ps, pr, ys, yr, rss, rsr, ts, tr,
+    ev, own_row, buck_row, cbias, cbuck, tb, gain, clen, wbuf, kb, kt, vb, s1, r1, s2, r2, s3, r3, s4, r4, qb, part, ss, rr, cr, nkt, newv, gates, cbh, nbh, mask,
+    in_sem, own_sem, kv_sem, xs, xr, zs, zr, ps, pr, bzs, bzr, bxs, bxr, bps, bpr, ys, yr, rss, rsr, ts, tr,
 ):
     u, c = lax.axis_index("users"), lax.axis_index("ctx")
     z, xc = lax.div(u, XC), lax.rem(u, XC)
@@ -47,32 +49,59 @@
             src_ref=src, dst_ref=dst, send_sem=send, recv_sem=recv, device_id=to, device_id_type=MESH
         )
 
+    def shard(m, begin=0, end=D):
+        return (wcs if m == 0 else wps).at[:, pl.ds((BEGINS[m] or 0) + begin, end - begin)]
+
+    def own_copy(m):
+        return pltpu.make_async_copy(shard(m), wbuf.at[m, z, x, k], own_sem.at[m])
+
     def xcopy(m, i):
-        ref = wbuf.at[m, z, x, k]
-        return remote(ref, ref, xs.at[m, i - 1], xr.at[m, i - 1], dev(z, lax.rem(x + i, NX), k))
+        to = dev(z, lax.rem(x + i, NX), k)
+        return remote(shard(m, 0, XF), wbuf.at[m, z, x, k, :, pl.ds(0, XF)], xs.at[m, i - 1], xr.at[m, i - 1], to)
 
     def zcopy(m, way, s, h):
         zz = lax.rem(z - s + NZ, NZ) if way == 0 else lax.rem(z + s, NZ)
         to = lax.rem(z + 1, NZ) if way == 0 else lax.rem(z + NZ - 1, NZ)
         i = 2 * s + h if s < 3 else 6
-        ref = wbuf.at[m, zz, pl.ds(2 * h, 2), k]
+        ref = wbuf.at[m, zz, pl.ds(2 * h, 2), k, :, pl.ds(0, XF)]
         return remote(ref, ref, zs.at[m, way, i], zr.at[m, way, i], dev(to, x, k))
 
     def pcopy(m, j):
-        ref = wbuf.at[m, lax.rem(z + j, NZ), :, k]
+        ref = wbuf.at[m, lax.rem(z + j, NZ), :, k, :, pl.ds(0, XF)]
         return remote(ref, ref, ps.at[m, j], pr.at[m, j], dev(z, x, 1 - k))
 
-    def x_start(m):
+    def bzcopy(m, i):
+        to = dev(lax.rem(z + i, NZ), x, k)
+        dst = wbuf.at[m, z, x, k, :, pl.ds(XF, D - XF)]
+        return remote(shard(m, XF, D), dst, bzs.at[m, i - 1], bzr.at[m, i - 1], to)
+
+    def bxcopy(m, i):
+        ref = wbuf.at[m, :, x, k, :, pl.ds(XF, D - XF)]
+        return remote(ref, ref, bxs.at[m, i - 1], bxr.at[m, i - 1], dev(z, lax.rem(x + i, NX), k))
+
+    def bpcopy(m, j):
+        ref = wbuf.at[m, :, lax.rem(x + j, NX), k, :, pl.ds(XF, D - XF)]
+        return remote(ref, ref, bps.at[m, j], bpr.at[m, j], dev(z, x, 1 - k))
+
+    def gather_start(m):
         for i in range(1, NX):
             xcopy(m, i).start()
-
-    def ring_begin(m):
+        for i in range(1, NZ):
+            bzcopy(m, i).start()
+
+    def gather_turn(m):
+        own_copy(m).wait()
         for i in range(1, NX):
             xcopy(m, i).wait_recv()
         for h in range(2):
             for way in range(2):
                 zcopy(m, way, 0, h).start()
         pcopy(m, 0).start()
+        for i in range(1, NZ):
+            bzcopy(m, i).wait_recv()
+        for i in range(1, NX):
+            bxcopy(m, i).start()
+        bpcopy(m, 0).start()
 
     def ring_step(m, s):
         for h in range(2):
@@ -87,14 +116,22 @@
             pcopy(m, 1 + s).start()
         else:
             pcopy(m, 4).start()
+            for i in range(1, NX):
+                bxcopy(m, i).wait_recv()
+                bpcopy(m, NX - i).start()
 
     def ring_end(m):
         for j in range(NZ):
             pcopy(m, j).wait_recv()
+        for j in range(NX):
+            bpcopy(m, j).wait_recv()
 
     def gather_sent(m):
         for i in range(1, NX):
             xcopy(m, i).wait_send()
+            bxcopy(m, i).wait_send()
+        for i in range(1, NZ):
+            bzcopy(m, i).wait_send()
         for way in range(2):
             for s in range(4):
                 for h in range(2):
@@ -102,6 +139,8 @@
                         zcopy(m, way, s, h).wait_send()
         for j in range(NZ):
             pcopy(m, j).wait_send()
+        for j in range(NX):
+            bpcopy(m, j).wait_send()
 
     def tcopy(leg, i):
         src, dst = ((s1, r1), (s2, r2), (s3, r3), (s4, r4))[leg]
@@ -127,14 +166,13 @@
         i = 2 * e + h if e < 3 else 6
         return remote(qb.at[si, h], qb.at[di, h], ys.at[way, i], yr.at[way, i], (u, to))
 
-    def y_stage(s):
-        for h in range(2):
-            for way in range(2):
-                if s == 3 and h != way:
-                    continue
-                ycopy(way, s, h).wait_recv()
-                if s < 2 or (s == 2 and h == way):
-                    ycopy(way, s + 1, h).start()
+    def y_chunk(s, h):
+        for way in range(2):
+            if s == 3 and h != way:
+                continue
+            ycopy(way, s, h).wait_recv()
+            if s < 2 or (s == 2 and h == way):
+                ycopy(way, s + 1, h).start()
 
     def scopy(way, d, h):
         to = c_down if way == 0 else c_up
@@ -150,7 +188,12 @@
         scopy(way, d, h).start()
 
     for m in range(5):
-        wbuf[m, z, x, k] = wcs[...] if m == 0 else wps[:, BEGINS[m] : BEGINS[m] + D]
+        own_copy(m).start()
+    small = ((owners, own_row), (buckets, buck_row), (cache_bucket, cbuck), (time_bias, tb), (length, clen),
+             (events, ev), (cross_bias, cbias), (norm_gain, gain))
+    small_in = [pltpu.make_async_copy(src, dst, in_sem.at[i]) for i, (src, dst) in enumerate(small)]
+    for copy in small_in:
+        copy.start()
     k_in = pltpu.make_async_copy(ck.at[0], kb, kv_sem.at[0])
     v_in = pltpu.make_async_copy(cv.at[0], vb, kv_sem.at[1])
     k_in.start()
@@ -164,10 +207,12 @@
         pl.semaphore_signal(barrier, inc=1, device_id=peer, device_id_type=MESH)
     pl.semaphore_wait(barrier, len(peers))
 
-    x_start(0)
-    x_start(1)
-
-    oc, orow = own_col[...], own_row[...]
+    gather_start(0)
+
+    for copy in small_in:
+        copy.wait()
+    orow = own_row[...]
+    oc = jnp.broadcast_to(orow.astype(F32), (ROWS, ROWS)).T.astype(I32)
     first = lax.broadcasted_iota(I32, (ROWS, ROWS), 0)
     second = lax.broadcasted_iota(I32, (ROWS, ROWS), 1)
     same = oc == orow
@@ -179,16 +224,19 @@
     label_block = jnp.broadcast_to(label, (SLOTS, HW)).astype(BF16)
     s1[:, :, D:] = label_block.reshape(NZ, 16, HW)
 
+    for n in range(4):
+        cols = slice(n * 256, (n + 1) * 256)
+        placed = jnp.dot(place, ev[:, cols], preferred_element_type=F32)
+        s1[:, :, cols] = placed.astype(BF16).reshape(NZ, 16, 256)
+    t_start(0)
+    gather_turn(0)
+    gather_start(1)
+
     to_slot = lax.broadcasted_iota(I32, (SLOTS, SLOTS), 0)
     from_slot = lax.broadcasted_iota(I32, (SLOTS, SLOTS), 1)
     swapped = ((to_slot >> 1) & 7) * 16 + (to_slot >> 4) * 2 + (to_slot & 1)
     swap = jnp.where(swapped == from_slot, 1.0, 0.0).astype(BF16)
 
-    ring_begin(0)
-
-    level = lax.broadcasted_iota(I32, (BUCKETS, CACHE), 0)
-    picked = jnp.where(level == cbuck[...], 1.0, 0.0)
-    cbh[...] = 0.5 * jnp.dot(tbt[...], picked, precision=lax.Precision.HIGHEST, preferred_element_type=F32)
     k_in.wait()
 
     def turn(h, _):
@@ -197,12 +245,19 @@
         return _
 
     lax.fori_loop(0, 3, turn, 0)
+    t_wait(0)
+    moved = jnp.dot(swap, r1[...].reshape(SLOTS, DL), preferred_element_type=F32)
+    s2[...] = moved.astype(BF16).reshape(XC, 16, DL)
+    t_start(1)
     ring_step(0, 0)
     lax.fori_loop(3, 6, turn, 0)
     ring_step(0, 1)
     lax.fori_loop(6, 8, turn, 0)
+    gather_turn(1)
+    gather_start(2)
+    ring_step(0, 2)
     v_in.wait()
-    live = clen[0] - c * CACHE
+    live = clen[...] - c * CACHE
 
     def blank(i, _):
         rows = pl.ds(pl.multiple_of(i * 128, 128), 128)
@@ -210,43 +265,34 @@
         vb[rows, :] = jnp.where(at < live, vb[rows, :].astype(F32), 0.0).astype(BF16)
         return _
 
-    ring_step(0, 2)
-    ring_begin(1)
     lax.fori_loop(0, CACHE // 128, blank, 0)
+    level = lax.broadcasted_iota(I32, (BUCKETS, CACHE), 0)
+    picked = jnp.where(level == cbuck[...], 1.0, 0.0)
+    bias_rows = tb[...]
+    cbh[...] = 0.5 * jnp.dot(bias_rows, picked, precision=lax.Precision.HIGHEST, preferred_element_type=F32)
+    ring_step(1, 0)
     ring_step(0, 3)
+    t_wait(1)
+    ring_step(1, 1)
+    gather_turn(2)
+    gather_start(3)
     ring_end(0)
 
     def times(rows_value, m, n):
         block = wbuf[m, :, :, :, :, n * 256 : (n + 1) * 256].reshape(D, 256)
         return jnp.dot(rows_value, block, preferred_element_type=F32)
 
-    event_rows = ev[...]
+    arrived = r2[:, :, :D].reshape(SLOTS, D)
     for n in range(4):
         cols = slice(n * 256, (n + 1) * 256)
-        source = event_rows[:, cols].astype(F32)
-        crossed = (source * (times(event_rows, 0, n) + cbias[:, cols]) + source).astype(BF16)
-        placed = jnp.dot(place, crossed, preferred_element_type=F32).astype(BF16)
-        s1[:, :, cols] = placed.reshape(NZ, 16, 256)
-    t_start(0)
-    x_start(2)
-    ring_step(1, 0)
-    t_wait(0)
-    moved = jnp.dot(swap, r1[...].reshape(SLOTS, DL), preferred_element_type=F32)
-    s2[...] = moved.astype(BF16).reshape(XC, 16, DL)
-    t_start(1)
-    ring_step(1, 1)
+        source = arrived[:, cols].astype(F32)
+        cr[:, cols] = (source * (times(arrived, 0, n) + cbias[:, cols]) + source).astype(BF16)
     ring_step(1, 2)
-    ring_begin(2)
     ring_step(1, 3)
-    x_start(3)
-    x_start(4)
-    t_wait(1)
     ring_end(1)
 
-    arrived = r2[:, :, :D].reshape(SLOTS, D)
-
     def projected(m, n):
-        return half_silu(0.5 * times(arrived, m, n))
+        return half_silu(0.5 * times(cr[...], m, n))
 
     for n in range(4):
         qb[0, n // 2, :, (n % 2) * 256 : (n % 2 + 1) * 256] = projected(1, n).astype(BF16)
@@ -256,15 +302,14 @@
 
     labels = r2[:, :, D:].reshape(SLOTS, HW).astype(F32).T[:BUCKETS]
     new_picked = jnp.where(labels == lax.broadcasted_iota(I32, (BUCKETS, SLOTS), 0).astype(F32), 1.0, 0.0)
-    nbh[...] = 0.5 * jnp.dot(tbt[...], new_picked, precision=lax.Precision.HIGHEST, preferred_element_type=F32)
+    nbh[...] = 0.5 * jnp.dot(bias_rows, new_picked, precision=lax.Precision.HIGHEST, preferred_element_type=F32)
 
     half_scale = 0.5 * HW ** (-0.5)
 
     def attend(blocks, half):
-        def one_head(i, _):
+        for i in range(4):
             h = half * 4 + i
-            lanes = pl.ds(pl.multiple_of(i * HW, HW), HW)
-            wide = pl.ds(pl.multiple_of(h * HW, HW), HW)
+            lanes, wide = pl.ds(i * HW, HW), pl.ds(h * HW, HW)
             q = jnp.concatenate([qb[d, half, :, lanes] for d in blocks], axis=0)
             s = jnp.dot(q, kt[wide, :], preferred_element_type=F32)
             s = s * half_scale + cbh[pl.ds(h, 1), :]
@@ -272,9 +317,6 @@
             o = jnp.dot(w, vb[:, wide], preferred_element_type=F32)
             for j, d in enumerate(blocks):
                 part[d, half, :, lanes] = o[j * SLOTS : (j + 1) * SLOTS]
-            return _
-
-        lax.fori_loop(0, 4, one_head, 0)
 
     def shard_of(slot):
         return ((slot >> 1) & 7) * XC + (slot >> 4)
@@ -287,67 +329,70 @@
 
     def attend_new(begin, end):
         count = end - begin
-
-        def one_head(h, _):
-            half = lax.div(h, 4)
-            lanes = pl.ds(pl.multiple_of(lax.rem(h, 4) * HW, HW), HW)
-            wide = pl.ds(pl.multiple_of(h * HW, HW), HW)
+        seen = mask[begin:end].reshape(count * SLOTS, SLOTS)
+        for h in range(HEADS):
+            half = h // 4
+            lanes, wide = pl.ds(h % 4 * HW, HW), pl.ds(h * HW, HW)
             q = qb[begin:end, half, :, lanes].reshape(count * SLOTS, HW)
-            s = lax.dot_general(q, newk[:, wide], (((1,), (1,)), ((), ())), preferred_element_type=F32)
+            s = jnp.dot(q, nkt[wide, :], preferred_element_type=F32)
             s = s * half_scale + nbh[pl.ds(h, 1), :]
-            w = (half_silu(s) * mask[begin:end].reshape(count * SLOTS, SLOTS)).astype(BF16)
+            w = (half_silu(s) * seen).astype(BF16)
             o = jnp.dot(w, newv[:, wide], preferred_element_type=F32)
             part[begin:end, half, :, lanes] += o.reshape(count, SLOTS, HW)
-            return _
-
-        lax.fori_loop(0, HEADS, one_head, 0)
 
     attend((0,), 0)
     ring_step(2, 0)
     attend((0,), 1)
-    y_stage(0)
+    y_chunk(0, 0)
     ring_step(2, 1)
+    gather_turn(3)
+    gather_start(4)
     attend((1, 7), 0)
+    y_chunk(0, 1)
     ring_step(2, 2)
-    ring_begin(3)
+    attend((1, 7), 1)
+    y_chunk(1, 0)
     ring_step(2, 3)
-    attend((1, 7), 1)
-    ring_end(2)
-    y_stage(1)
-    for n in range(4):
-        newk[:, n * 256 : (n + 1) * 256] = projected(2, n).astype(BF16)
     ring_step(3, 0)
     attend((2, 6), 0)
+    y_chunk(1, 1)
     ring_step(3, 1)
+    gather_turn(4)
     attend((2, 6), 1)
-    y_stage(2)
+    y_chunk(2, 0)
     ring_step(3, 2)
-    ring_begin(4)
+    ring_end(2)
+    for n in range(4):
+        nkt[n * 256 : (n + 1) * 256, :] = projected(2, n).astype(BF16).T
     attend((3, 5), 0)
+    y_chunk(2, 1)
     ring_step(3, 3)
+    ring_step(4, 0)
     attend((3, 5), 1)
     ring_end(3)
     for n in range(4):
         newv[:, n * 256 : (n + 1) * 256] = projected(3, n).astype(BF16)
-    attend_new(5, 8)
-    attend_new(0, 4)
+    attend_new(3, 4)
+    attend_new(5, 6)
     rs_send(0, 3, 1)
     rs_send(1, 3, 0)
-    y_stage(3)
+    y_chunk(3, 0)
     attend((4,), 0)
+    ring_step(4, 1)
+    y_chunk(3, 1)
     attend((4,), 1)
     attend_new(4, 5)
     rs_send(0, 4, 0)
     rs_send(1, 4, 1)
-    ring_step(4, 0)
+    ring_step(4, 2)
+    attend_new(6, 8)
+    attend_new(0, 3)
     rs_send(0, 3, 0)
     rs_send(1, 3, 1)
-    ring_step(4, 1)
+    ring_step(4, 3)
     for h in range(2):
         rs_send(0, 2, 1 - h)
         rs_send(1, 2, h)
-    ring_step(4, 2)
-    ring_step(4, 3)
     ring_end(4)
     for n in range(4):
         gates[:, n * 256 : (n + 1) * 256] = projected(4, n).astype(BF16)
@@ -373,9 +418,7 @@
     moved_back = jnp.dot(swap, r3[...].reshape(SLOTS, D), preferred_element_type=F32)
     s4[...] = moved_back.astype(BF16).reshape(NZ, 16, D)
     t_start(3)
-    rank_col = jnp.sum(jnp.where((own_col[...] == own_row[...]) & (second < first), 1.0, 0.0), axis=1, keepdims=True)
-    slot_col = own_col[...] * 2 + rank_col.astype(I32)
-    unplace = jnp.where(lax.broadcasted_iota(I32, (ROWS, SLOTS), 1) == slot_col, 1.0, 0.0).astype(BF16)
+    unplace = place.astype(F32).T.astype(BF16)
     for m in range(5):
         gather_sent(m)
     for way in range(2):
@@ -398,15 +441,22 @@
     cache_keys, cache_values, cache_length, cache_bucket, time_bias, norm_gain,
 ):
     vmem = pl.BlockSpec(memory_space=pltpu.VMEM)
-    whole = pl.BlockSpec(memory_space=pl.ANY)
-    smem = pl.BlockSpec(memory_space=pltpu.SMEM)
+    whole = pl.BlockSpec(memory_space=pltpu.HBM)
     dma = pltpu.SemaphoreType.DMA
     return pl.pallas_call(
         kernel,
         out_shape=jax.ShapeDtypeStruct((ROWS, D), BF16),
-        in_specs=[vmem] * 7 + [whole] * 2 + [smem] + [vmem] * 3,
+        in_specs=[whole] * 12,
         out_specs=vmem,
         scratch_shapes=[
+            pltpu.VMEM((ROWS, D), BF16),
+            pltpu.VMEM((1, ROWS), I32),
+            pltpu.VMEM((1, ROWS), I32),
+            pltpu.VMEM((1, D), F32),
+            pltpu.VMEM((1, CACHE), I32),
+            pltpu.VMEM((HEADS, BUCKETS), F32),
+            pltpu.VMEM((1, D), F32),
+            pltpu.VMEM((1, 1), I32),
             pltpu.VMEM((5, NZ, NX, 2, 16, D), BF16),
             pltpu.VMEM((CACHE, D), BF16),
             pltpu.VMEM((D, CACHE), BF16),
@@ -424,11 +474,14 @@
             pltpu.VMEM((2, 4, 2, SLOTS, 512), BF16),
             pltpu.VMEM((2, 4, 2, SLOTS, 512), BF16),
             pltpu.VMEM((SLOTS, D), BF16),
+            pltpu.VMEM((D, SLOTS), BF16),
             pltpu.VMEM((SLOTS, D), BF16),
             pltpu.VMEM((SLOTS, D), BF16),
             pltpu.VMEM((HEADS, CACHE), F32),
             pltpu.VMEM((HEADS, SLOTS), F32),
             pltpu.VMEM((NY, SLOTS, SLOTS), F32),
+            dma((8,)),
+            dma((5,)),
             dma((2,)),
             dma((5, 3)),
             dma((5, 3)),
@@ -436,6 +489,12 @@
             dma((5, 2, 7)),
             dma((5, 8)),
             dma((5, 8)),
+            dma((5, 7)),
+            dma((5, 7)),
+            dma((5, 3)),
+            dma((5, 3)),
+            dma((5, 4)),
+            dma((5, 4)),
             dma((2, 7)),
             dma((2, 7)),
             dma((2, 7)),
@@ -444,12 +503,11 @@
             dma((4, 7)),
         ],
         compiler_params=pltpu.CompilerParams(
-            collective_id=0, has_side_effects=True, vmem_limit_bytes=48 * 1024 * 1024
+            collective_id=0, has_side_effects=True, vmem_limit_bytes=VMEM_BYTES
         ),
         name="ingest",
     )(
         events,
-        owner_id,
         owner_id.reshape(1, ROWS),
         event_bucket.reshape(1, ROWS),
         cross_weight,
@@ -457,7 +515,7 @@
         cross_bias.reshape(1, D),
         cache_keys,
         cache_values,
-        cache_length,
+        cache_length.reshape(1, 1),
         cache_bucket,
         time_bias.T,
         norm_gain.reshape(1, D),

time: 159 us -> 122 us (0.77); the launches traced: 157 us -> 122 us
  Pallas kernels: 145 us -> 120 us
  local copies, waits for them, and re-layouts: 11.2 us -> 1.57 us
    pallas_call x1, Pallas kernels: 145 us -> 120 us  [shards(): pl.pallas_call(kernel, out_shape=jax.ShapeDtypeStruct((ROWS, D), BF16), i...]
    unnamed x24 -> x1, local copies, waits for them, and re-layouts: 11.2 us -> 1.57 us
where the time goes in v2:
time: 122 us
  Pallas kernels  120 us (98%)
  local copies, waits for them, and re-layouts  1.57 us (1%)
    pallas_call x1, Pallas kernels, shards(): pl.pallas_call(kernel, out_shape=jax.ShapeDtypeStruct((ROWS, D), BF16), i...  120 us

profile of v2, /device:TPU:1, one launch (start us, length us, event | category | flops | bytes accessed | tf_op | source)
XLA Modules:
  0.0 121.8 jit_solution(9087949251645647875)
XLA Ops:
  0.7 119.6 %ingest.1 = bf16[64,1024]{1,0:T(8,128)(2,1)} custom-call(bf16[64,1024]{1,0:T(8,128)(2,1)} %events.1, s32[1,64]{1,0:T(1,128)} %bitcast.10, s32[1,64]{1,0:T(1,128)} %bitcast.11, bf16[16,1024]{1,0:T(8,128)(2,1)} %wcs.1, bf16[16,4096]{1,0:T(8,128)(2,1)} %wps.1, f32[1,1024]{1,0:T(1,128)} %bitcast.7, bf16[1,1024,1024]{2,1,0:T(8,128)(2,1)} %ck.1, ...), custom_call_target="tpu_custom_call" | custom-call | tf_op jit(solution)/shard_map/ingest/pallas_call | solution.py:446
  120.2 1.6 %copy.15 = bf16[64,1024]{1,0:T(8,128)(2,1)} copy(bf16[64,1024]{1,0:T(8,128)(2,1)} %ingest.1) | data formatting | bytes 262144

commit v3 on v2

--- a/solution.py
+++ b/solution.py
@@ -21,7 +21,8 @@
 HW = 128
 BUCKETS = 32
 EPS = 1e-05
-XF = 384
+XF = 256
+FAR_FIRST = (4, 3, 5, 2, 6, 1, 7)
 VMEM_BYTES = 60 * 1024 * 1024
 BEGINS = (None, 2048, 3072, 1024, 0)
 
@@ -33,8 +34,8 @@
 def kernel(
     events, owners, buckets, wcs, wps, cross_bias, ck, cv, length, cache_bucket, time_bias, norm_gain,
     out,
-    ev, own_row, buck_row, cbias, cbuck, tb, gain, clen, wbuf, kb, kt, vb, s1, r1, s2, r2, s3, r3, s4, r4, qb, part, ss, rr, cr, nkt, newv, gates, cbh, nbh, mask,
-    in_sem, own_sem, kv_sem, xs, xr, zs, zr, ps, pr, bzs, bzr, bxs, bxr, bps, bpr, ys, yr, rss, rsr, ts, tr,
+    ev, own_row, buck_row, cbias, cbuck, tb, gain, clen, wa, wb, wq, kb, kt, vb, s1, r1, s2, r2, s3, r3, s4, r4, s5, r5, s6, r6, qb, part, ss, rr, cr, nkt, newv, gates, cbh, nbh, mask,
+    in_sem, own_sem, kv_sem, xs, xr, zs, zr, ps, pr, bzs, bzr, bxs, bxr, bps, bpr, qo, qzs, qzr, qxs, qxr, qys, qyr, qps, qpr, ys, yr, rss, rsr, ts, tr,
 ):
     u, c = lax.axis_index("users"), lax.axis_index("ctx")
     z, xc = lax.div(u, XC), lax.rem(u, XC)
@@ -49,78 +50,74 @@
             src_ref=src, dst_ref=dst, send_sem=send, recv_sem=recv, device_id=to, device_id_type=MESH
         )
 
-    def shard(m, begin=0, end=D):
+    def shard(m, begin, end):
         return (wcs if m == 0 else wps).at[:, pl.ds((BEGINS[m] or 0) + begin, end - begin)]
 
-    def own_copy(m):
-        return pltpu.make_async_copy(shard(m), wbuf.at[m, z, x, k], own_sem.at[m])
+    def own_copies(m):
+        return (
+            pltpu.make_async_copy(shard(m, 0, XF), wa.at[m, k, z, x], own_sem.at[m, 0]),
+            pltpu.make_async_copy(shard(m, XF, D), wb.at[m, k, x, z], own_sem.at[m, 1]),
+        )
 
     def xcopy(m, i):
         to = dev(z, lax.rem(x + i, NX), k)
-        return remote(shard(m, 0, XF), wbuf.at[m, z, x, k, :, pl.ds(0, XF)], xs.at[m, i - 1], xr.at[m, i - 1], to)
-
-    def zcopy(m, way, s, h):
-        zz = lax.rem(z - s + NZ, NZ) if way == 0 else lax.rem(z + s, NZ)
-        to = lax.rem(z + 1, NZ) if way == 0 else lax.rem(z + NZ - 1, NZ)
-        i = 2 * s + h if s < 3 else 6
-        ref = wbuf.at[m, zz, pl.ds(2 * h, 2), k, :, pl.ds(0, XF)]
-        return remote(ref, ref, zs.at[m, way, i], zr.at[m, way, i], dev(to, x, k))
+        return remote(shard(m, 0, XF), wa.at[m, k, z, x], xs.at[m, i - 1], xr.at[m, i - 1], to)
+
+    def zcopy(m, i):
+        ref = wa.at[m, k, z]
+        return remote(ref, ref, zs.at[m, i - 1], zr.at[m, i - 1], dev(lax.rem(z + i, NZ), x, k))
 
     def pcopy(m, j):
-        ref = wbuf.at[m, lax.rem(z + j, NZ), :, k, :, pl.ds(0, XF)]
+        ref = wa.at[m, k, lax.rem(z + j, NZ)]
         return remote(ref, ref, ps.at[m, j], pr.at[m, j], dev(z, x, 1 - k))
 
     def bzcopy(m, i):
         to = dev(lax.rem(z + i, NZ), x, k)
-        dst = wbuf.at[m, z, x, k, :, pl.ds(XF, D - XF)]
-        return remote(shard(m, XF, D), dst, bzs.at[m, i - 1], bzr.at[m, i - 1], to)
+        return remote(shard(m, XF, D), wb.at[m, k, x, z], bzs.at[m, i - 1], bzr.at[m, i - 1], to)
 
     def bxcopy(m, i):
-        ref = wbuf.at[m, :, x, k, :, pl.ds(XF, D - XF)]
+        ref = wb.at[m, k, x]
         return remote(ref, ref, bxs.at[m, i - 1], bxr.at[m, i - 1], dev(z, lax.rem(x + i, NX), k))
 
     def bpcopy(m, j):
-        ref = wbuf.at[m, :, lax.rem(x + j, NX), k, :, pl.ds(XF, D - XF)]
+        ref = wb.at[m, k, lax.rem(x + j, NX)]
         return remote(ref, ref, bps.at[m, j], bpr.at[m, j], dev(z, x, 1 - k))
 
     def gather_start(m):
-        for i in range(1, NX):
+        for i in (2, 1, 3):
             xcopy(m, i).start()
-        for i in range(1, NZ):
+        for i in FAR_FIRST:
             bzcopy(m, i).start()
 
     def gather_turn(m):
-        own_copy(m).wait()
+        turn_first(m)
+        turn_others(m)
+
+    def turn_first(m):
+        for copy in own_copies(m):
+            copy.wait()
         for i in range(1, NX):
             xcopy(m, i).wait_recv()
-        for h in range(2):
-            for way in range(2):
-                zcopy(m, way, 0, h).start()
+        for i in FAR_FIRST:
+            zcopy(m, i).start()
         pcopy(m, 0).start()
+
+    def turn_others(m):
         for i in range(1, NZ):
             bzcopy(m, i).wait_recv()
-        for i in range(1, NX):
+        for i in (2, 1, 3):
             bxcopy(m, i).start()
         bpcopy(m, 0).start()
 
-    def ring_step(m, s):
-        for h in range(2):
-            for way in range(2):
-                if s == 3 and h != way:
-                    continue
-                zcopy(m, way, s, h).wait_recv()
-                if s < 2 or (s == 2 and h == way):
-                    zcopy(m, way, s + 1, h).start()
-        if s < 3:
-            pcopy(m, 7 - s).start()
-            pcopy(m, 1 + s).start()
-        else:
-            pcopy(m, 4).start()
-            for i in range(1, NX):
-                bxcopy(m, i).wait_recv()
-                bpcopy(m, NX - i).start()
-
-    def ring_end(m):
+    def gather_pass(m):
+        for i in FAR_FIRST:
+            zcopy(m, i).wait_recv()
+            pcopy(m, NZ - i).start()
+        for i in (1, 3, 2):
+            bxcopy(m, i).wait_recv()
+            bpcopy(m, NX - i).start()
+
+    def gather_end(m):
         for j in range(NZ):
             pcopy(m, j).wait_recv()
         for j in range(NX):
@@ -132,29 +129,105 @@
             bxcopy(m, i).wait_send()
         for i in range(1, NZ):
             bzcopy(m, i).wait_send()
+            zcopy(m, i).wait_send()
+        for j in range(NZ):
+            pcopy(m, j).wait_send()
+        for j in range(NX):
+            bpcopy(m, j).wait_send()
+
+    def q_own():
+        return pltpu.make_async_copy(shard(1, 0, D), wq.at[k, c, x], qo)
+
+    def qzcopy(i):
+        return remote(shard(1, 0, D), wq.at[k, c, x], qzs.at[i - 1], qzr, dev(lax.rem(z + i, NZ), x, k))
+
+    def qxcopy(i):
+        ref = wq.at[k, c, x]
+        return remote(ref, ref, qxs.at[i - 1], qxr.at[i - 1], dev(z, lax.rem(x + i, NX), k))
+
+    def qycopy(way, s, h):
+        origin = lax.rem(c - s + NY, NY) if way == 0 else lax.rem(c + s, NY)
+        i = 2 * s + h if s < 3 else 6
+        ref = wq.at[k, origin, pl.ds(2 * h, 2)]
+        return remote(ref, ref, qys.at[way, i], qyr.at[way, i], (u, c_up if way == 0 else c_down))
+
+    def qpcopy(j):
+        ref = wq.at[k, lax.rem(c + j, NY)]
+        return remote(ref, ref, qps.at[j], qpr.at[j], dev(z, x, 1 - k))
+
+    def q_start():
+        @pl.when(z == c)
+        def _():
+            q_own().start()
+            for i in FAR_FIRST:
+                qzcopy(i).start()
+
+    def q_turn():
+        @pl.when(z == c)
+        def _():
+            q_own().wait()
+
+        @pl.when(z != c)
+        def _():
+            qzcopy(1).wait_recv()
+
+        for i in (2, 1, 3):
+            qxcopy(i).start()
+
+    def q_begin():
+        for i in range(1, NX):
+            qxcopy(i).wait_recv()
+        for h in range(2):
+            for way in range(2):
+                qycopy(way, 0, h).start()
+        qpcopy(0).start()
+
+    def q_step(s):
+        for h in range(2):
+            for way in range(2):
+                if s == 3 and h != way:
+                    continue
+                qycopy(way, s, h).wait_recv()
+                if s < 2 or (s == 2 and h == way):
+                    qycopy(way, s + 1, h).start()
+        for j in (7 - s, 1 + s) if s < 3 else (4,):
+            qpcopy(j).start()
+
+    def q_end():
+        for j in range(NY):
+            qpcopy(j).wait_recv()
+
+    def q_sent():
+        @pl.when(z == c)
+        def _():
+            for i in range(1, NZ):
+                qzcopy(i).wait_send()
+
+        for i in range(1, NX):
+            qxcopy(i).wait_send()
         for way in range(2):
             for s in range(4):
                 for h in range(2):
                     if s < 3 or h == way:
-                        zcopy(m, way, s, h).wait_send()
-        for j in range(NZ):
-            pcopy(m, j).wait_send()
-        for j in range(NX):
-            bpcopy(m, j).wait_send()
+                        qycopy(way, s, h).wait_send()
+        for j in range(NY):
+            qpcopy(j).wait_send()
+
+    legs = ((s1, r1), (s2, r2), (s3, r3), (s4, r4), (s5, r5), (s6, r6))
 
     def tcopy(leg, i):
-        src, dst = ((s1, r1), (s2, r2), (s3, r3), (s4, r4))[leg]
-        if leg in (0, 3):
+        src, dst = legs[leg]
+        if leg in (0, 3, 4):
             to = lax.rem(z + i, NZ)
             return remote(src.at[to], dst.at[z], ts.at[leg, i - 1], tr.at[leg, i - 1], dev(to, x, k))
         to = lax.rem(xc + i, XC)
         return remote(src.at[to], dst.at[xc], ts.at[leg, i - 1], tr.at[leg, i - 1], (z * XC + to, c))
 
     def t_start(leg):
-        for i in range(1, 8):
+        for i in FAR_FIRST:
             tcopy(leg, i).start()
-        src, dst = ((s1, r1), (s2, r2), (s3, r3), (s4, r4))[leg]
-        mine = z if leg in (0, 3) else xc
+        src, dst = legs[leg]
+        mine = z if leg in (0, 3, 4) else xc
         dst[mine] = src[mine]
 
     def t_wait(leg):
@@ -187,8 +260,9 @@
         ss[way, d - 1, h] = v.astype(BF16)
         scopy(way, d, h).start()
 
-    for m in range(5):
-        own_copy(m).start()
+    for m in (0, 2, 3, 4):
+        for copy in own_copies(m):
+            copy.start()
     small = ((owners, own_row), (buckets, buck_row), (cache_bucket, cbuck), (time_bias, tb), (length, clen),
              (events, ev), (cross_bias, cbias), (norm_gain, gain))
     small_in = [pltpu.make_async_copy(src, dst, in_sem.at[i]) for i, (src, dst) in enumerate(small)]
@@ -207,6 +281,7 @@
         pl.semaphore_signal(barrier, inc=1, device_id=peer, device_id_type=MESH)
     pl.semaphore_wait(barrier, len(peers))
 
+    q_start()
     gather_start(0)
 
     for copy in small_in:
@@ -229,8 +304,10 @@
         placed = jnp.dot(place, ev[:, cols], preferred_element_type=F32)
         s1[:, :, cols] = placed.astype(BF16).reshape(NZ, 16, 256)
     t_start(0)
-    gather_turn(0)
-    gather_start(1)
+    q_turn()
+    turn_first(0)
+    q_begin()
+    turn_others(0)
 
     to_slot = lax.broadcasted_iota(I32, (SLOTS, SLOTS), 0)
     from_slot = lax.broadcasted_iota(I32, (SLOTS, SLOTS), 1)
@@ -244,18 +321,17 @@
         kt[lanes, :] = kb[:, lanes].T
         return _
 
+    q_step(0)
     lax.fori_loop(0, 3, turn, 0)
+    q_step(1)
     t_wait(0)
     moved = jnp.dot(swap, r1[...].reshape(SLOTS, DL), preferred_element_type=F32)
     s2[...] = moved.astype(BF16).reshape(XC, 16, DL)
     t_start(1)
-    ring_step(0, 0)
-    lax.fori_loop(3, 6, turn, 0)
-    ring_step(0, 1)
-    lax.fori_loop(6, 8, turn, 0)
-    gather_turn(1)
     gather_start(2)
-    ring_step(0, 2)
+    q_step(2)
+    lax.fori_loop(3, 8, turn, 0)
+    q_step(3)
     v_in.wait()
     live = clen[...] - c * CACHE
 
@@ -270,16 +346,21 @@
     picked = jnp.where(level == cbuck[...], 1.0, 0.0)
     bias_rows = tb[...]
     cbh[...] = 0.5 * jnp.dot(bias_rows, picked, precision=lax.Precision.HIGHEST, preferred_element_type=F32)
-    ring_step(1, 0)
-    ring_step(0, 3)
-    t_wait(1)
-    ring_step(1, 1)
+    gather_pass(0)
     gather_turn(2)
     gather_start(3)
-    ring_end(0)
+    t_wait(1)
+    gather_end(0)
 
     def times(rows_value, m, n):
-        block = wbuf[m, :, :, :, :, n * 256 : (n + 1) * 256].reshape(D, 256)
+        blocks = []
+        for u_ in range(NZ * XC):
+            z_, x_, k_ = u_ // XC, u_ // 2 % NX, u_ % 2
+            if m == 1:
+                blocks.append(wq[k_, z_, x_, :, n * 256 : (n + 1) * 256])
+                continue
+            blocks.append(wa[m, k_, z_, x_] if n == 0 else wb[m, k_, x_, z_, :, n * 256 - XF : (n + 1) * 256 - XF])
+        block = jnp.concatenate(blocks, axis=0)
         return jnp.dot(rows_value, block, preferred_element_type=F32)
 
     arrived = r2[:, :, :D].reshape(SLOTS, D)
@@ -287,9 +368,7 @@
         cols = slice(n * 256, (n + 1) * 256)
         source = arrived[:, cols].astype(F32)
         cr[:, cols] = (source * (times(arrived, 0, n) + cbias[:, cols]) + source).astype(BF16)
-    ring_step(1, 2)
-    ring_step(1, 3)
-    ring_end(1)
+    q_end()
 
     def projected(m, n):
         return half_silu(0.5 * times(cr[...], m, n))
@@ -341,35 +420,28 @@
             part[begin:end, half, :, lanes] += o.reshape(count, SLOTS, HW)
 
     attend((0,), 0)
-    ring_step(2, 0)
     attend((0,), 1)
-    y_chunk(0, 0)
-    ring_step(2, 1)
     gather_turn(3)
     gather_start(4)
+    y_chunk(0, 0)
     attend((1, 7), 0)
     y_chunk(0, 1)
-    ring_step(2, 2)
+    gather_pass(2)
     attend((1, 7), 1)
     y_chunk(1, 0)
-    ring_step(2, 3)
-    ring_step(3, 0)
     attend((2, 6), 0)
+    gather_turn(4)
     y_chunk(1, 1)
-    ring_step(3, 1)
-    gather_turn(4)
     attend((2, 6), 1)
-    y_chunk(2, 0)
-    ring_step(3, 2)
-    ring_end(2)
+    gather_end(2)
     for n in range(4):
         nkt[n * 256 : (n + 1) * 256, :] = projected(2, n).astype(BF16).T
+    y_chunk(2, 0)
     attend((3, 5), 0)
     y_chunk(2, 1)
-    ring_step(3, 3)
-    ring_step(4, 0)
+    gather_pass(3)
     attend((3, 5), 1)
-    ring_end(3)
+    gather_end(3)
     for n in range(4):
         newv[:, n * 256 : (n + 1) * 256] = projected(3, n).astype(BF16)
     attend_new(3, 4)
@@ -377,28 +449,28 @@
     rs_send(0, 3, 1)
     rs_send(1, 3, 0)
     y_chunk(3, 0)
+    y_chunk(3, 1)
     attend((4,), 0)
-    ring_step(4, 1)
-    y_chunk(3, 1)
     attend((4,), 1)
     attend_new(4, 5)
     rs_send(0, 4, 0)
     rs_send(1, 4, 1)
-    ring_step(4, 2)
     attend_new(6, 8)
+    rs_send(1, 2, 0)
     attend_new(0, 3)
+    rs_send(0, 2, 1)
     rs_send(0, 3, 0)
     rs_send(1, 3, 1)
-    ring_step(4, 3)
-    for h in range(2):
-        rs_send(0, 2, 1 - h)
-        rs_send(1, 2, h)
-    ring_end(4)
+    gather_pass(4)
+    rs_send(0, 2, 0)
+    rs_send(1, 2, 1)
+    rs_send(0, 1, 1)
+    rs_send(1, 1, 0)
+    gather_end(4)
     for n in range(4):
         gates[:, n * 256 : (n + 1) * 256] = projected(4, n).astype(BF16)
-    for h in range(2):
-        rs_send(0, 1, 1 - h)
-        rs_send(1, 1, h)
+    rs_send(0, 1, 0)
+    rs_send(1, 1, 1)
 
     for h in range(2):
         for way in range(2):
@@ -408,32 +480,42 @@
     centered = [v - total / D for v in attended]
     squares = sum(jnp.sum(v * v, axis=1, keepdims=True) for v in centered)
     inverse = lax.rsqrt(squares / D + EPS)
+    gated = []
     for h in range(2):
         cols = slice(h * 512, (h + 1) * 512)
-        gated = centered[h] * inverse * gain[:, cols] * gates[:, cols].astype(F32)
-        s3[:, :, cols] = gated.astype(BF16).reshape(XC, 16, 512)
-
+        gated.append((centered[h] * inverse * gain[:, cols] * gates[:, cols].astype(F32)).astype(BF16))
+
+    def swapped_rows(value):
+        return jnp.dot(swap, value, preferred_element_type=F32).astype(BF16)
+
+    s5[...] = swapped_rows(gated[1]).reshape(NZ, 16, 512)
+    t_start(4)
+    s3[...] = gated[0].reshape(XC, 16, 512)
     t_start(2)
+    unplace = place.astype(F32).T.astype(BF16)
+    unplace_swapped = jnp.dot(unplace, swap, preferred_element_type=F32).astype(BF16)
+    q_sent()
+    for m in (0, 2, 3, 4):
+        gather_sent(m)
     t_wait(2)
-    moved_back = jnp.dot(swap, r3[...].reshape(SLOTS, D), preferred_element_type=F32)
-    s4[...] = moved_back.astype(BF16).reshape(NZ, 16, D)
+    s4[...] = swapped_rows(r3[...].reshape(SLOTS, 512)).reshape(NZ, 16, 512)
     t_start(3)
-    unplace = place.astype(F32).T.astype(BF16)
-    for m in range(5):
-        gather_sent(m)
+    t_wait(4)
+    s6[...] = swapped_rows(r5[...].reshape(SLOTS, 512)).reshape(XC, 16, 512)
+    t_start(5)
     for way in range(2):
         for e in range(4):
             for h in range(2):
                 if e < 3 or h == way:
                     ycopy(way, e, h).wait_send()
                     scopy(way, e + 1, h).wait_send()
-    for leg in range(3):
+    t_wait(3)
+    out[:, :512] = jnp.dot(unplace, r4[...].reshape(SLOTS, 512), preferred_element_type=F32).astype(BF16)
+    t_wait(5)
+    out[:, 512:] = jnp.dot(unplace_swapped, r6[...].reshape(SLOTS, 512), preferred_element_type=F32).astype(BF16)
+    for leg in range(6):
         for i in range(1, 8):
             tcopy(leg, i).wait_send()
-    t_wait(3)
-    out[...] = jnp.dot(unplace, r4[...].reshape(SLOTS, D), preferred_element_type=F32).astype(BF16)
-    for i in range(1, 8):
-        tcopy(3, i).wait_send()
 
 
 def shards(
@@ -457,7 +539,9 @@
             pltpu.VMEM((HEADS, BUCKETS), F32),
             pltpu.VMEM((1, D), F32),
             pltpu.VMEM((1, 1), I32),
-            pltpu.VMEM((5, NZ, NX, 2, 16, D), BF16),
+            pltpu.VMEM((5, 2, NZ, NX, 16, XF), BF16),
+            pltpu.VMEM((5, 2, NX, NZ, 16, D - XF), BF16),
+            pltpu.VMEM((2, NZ, NX, 16, D), BF16),
             pltpu.VMEM((CACHE, D), BF16),
             pltpu.VMEM((D, CACHE), BF16),
             pltpu.VMEM((CACHE, D), BF16),
@@ -465,10 +549,7 @@
             pltpu.VMEM((NZ, 16, DL), BF16),
             pltpu.VMEM((XC, 16, DL), BF16),
             pltpu.VMEM((XC, 16, DL), BF16),
-            pltpu.VMEM((XC, 16, D), BF16),
-            pltpu.VMEM((XC, 16, D), BF16),
-            pltpu.VMEM((NZ, 16, D), BF16),
-            pltpu.VMEM((NZ, 16, D), BF16),
+            *[pltpu.VMEM((8, 16, 512), BF16)] * 8,
             pltpu.VMEM((NY, 2, SLOTS, 512), BF16),
             pltpu.VMEM((NY, 2, SLOTS, 512), F32),
             pltpu.VMEM((2, 4, 2, SLOTS, 512), BF16),
@@ -481,12 +562,12 @@
             pltpu.VMEM((HEADS, SLOTS), F32),
             pltpu.VMEM((NY, SLOTS, SLOTS), F32),
             dma((8,)),
-            dma((5,)),
+            dma((5, 2)),
             dma((2,)),
             dma((5, 3)),
             dma((5, 3)),
-            dma((5, 2, 7)),
-            dma((5, 2, 7)),
+            dma((5, 7)),
+            dma((5, 7)),
             dma((5, 8)),
             dma((5, 8)),
             dma((5, 7)),
@@ -495,12 +576,21 @@
             dma((5, 3)),
             dma((5, 4)),
             dma((5, 4)),
+            dma,
+            dma((7,)),
+            dma,
+            dma((3,)),
+            dma((3,)),
+            dma((2, 7)),
+            dma((2, 7)),
+            dma((8,)),
+            dma((8,)),
             dma((2, 7)),
             dma((2, 7)),
             dma((2, 7)),
             dma((2, 7)),
-            dma((4, 7)),
-            dma((4, 7)),
+            dma((6, 7)),
+            dma((6, 7)),
         ],
         compiler_params=pltpu.CompilerParams(
             collective_id=0, has_side_effects=True, vmem_limit_bytes=VMEM_BYTES

time: 122 us -> 115 us (0.943)
  Pallas kernels: 120 us -> 112 us
    pallas_call x1, Pallas kernels: 120 us -> 112 us  [shards(): pl.pallas_call(kernel, out_shape=jax.ShapeDtypeStruct((ROWS, D), BF16), i...]
where the time goes in v3:
time: 115 us; the launch traced here: 114 us
  Pallas kernels  112 us (97%)
  local copies, waits for them, and re-layouts  1.57 us (1%)
    pallas_call x1, Pallas kernels, shards(): pl.pallas_call(kernel, out_shape=jax.ShapeDtypeStruct((ROWS, D), BF16), i...  112 us

profile of v3, /device:TPU:1, one launch (start us, length us, event | category | flops | bytes accessed | tf_op | source)
XLA Modules:
  0.0 114.1 jit_solution(8047360673840732923)
XLA Ops:
  0.7 111.9 %ingest.1 = bf16[64,1024]{1,0:T(8,128)(2,1)} custom-call(bf16[64,1024]{1,0:T(8,128)(2,1)} %events.1, s32[1,64]{1,0:T(1,128)} %bitcast.10, s32[1,64]{1,0:T(1,128)} %bitcast.11, bf16[16,1024]{1,0:T(8,128)(2,1)} %wcs.1, bf16[16,4096]{1,0:T(8,128)(2,1)} %wps.1, f32[1,1024]{1,0:T(1,128)} %bitcast.7, bf16[1,1024,1024]{2,1,0:T(8,128)(2,1)} %ck.1, ...), custom_call_target="tpu_custom_call" | custom-call | tf_op jit(solution)/shard_map/ingest/pallas_call | solution.py:528
  112.6 1.6 %copy.15 = bf16[64,1024]{1,0:T(8,128)(2,1)} copy(bf16[64,1024]{1,0:T(8,128)(2,1)} %ingest.1) | data formatting | bytes 262144
